TPU v7x, 32 devices: a whole 2x2x4 slice. The times are simulated.
32 devices in a mesh: groups: 2 (over y), graph: 4 (over z), dp: 4 (over x, core).
Axes of the slice: x: 2, y: 2, z: 4, core: 2. Of those that a mesh axis runs over, the one named last changes fastest.
Arguments:
- node_feats: bfloat16 [8, 192, 9, 512], P(('groups', 'dp'), 'graph'), parts along dimension 0, may hold values from -6 to 6
- frac_pos: float32 [8, 3, 192], P(('groups', 'dp'), None, 'graph'), parts along dimension 0, may hold values from 0 to 1
- lattice: float32 [8, 3, 3], P(('groups', 'dp')), parts along dimension 0, may hold values from -1 to 10, as said below
- edge_count: int32 [8, 4], P(('groups', 'dp'), 'graph'), parts along dimension 0, may hold values from 32 to 256, as said below
- edge_target: int32 [8, 1024], P(('groups', 'dp'), 'graph'), parts along dimension 0, may hold values from 0 to 47
- edge_source: int32 [8, 1024], P(('groups', 'dp'), 'graph'), parts along dimension 0, may hold values from 0 to 191, as said below
- edge_shift: int32 [8, 3, 1024], P(('groups', 'dp'), None, 'graph'), parts along dimension 0, may hold values from -1 to 1
- cotangent: bfloat16 [8, 192, 9, 512], P(('groups', 'dp'), 'graph'), parts along dimension 0, may hold values from -6 to 6
- w_in: bfloat16 [512, 512], P('dp'), may hold values from -0.25 to 0.25
- w_out: bfloat16 [512, 512], P('dp'), may hold values from -0.25 to 0.25
- w_rad: bfloat16 [128, 1536], P('dp'), may hold values from -3 to 3
Outputs:
- new_feats: bfloat16 [8, 192, 9, 512], P(('groups', 'dp'), 'graph'), parts along dimension 0
- grad_feats: bfloat16 [8, 192, 9, 512], P(('groups', 'dp'), 'graph'), parts along dimension 0
- grad_w_in: float32 [1024, 512], P(('groups', 'dp')), parts along dimension 0
- grad_w_out: float32 [1024, 512], P(('groups', 'dp')), parts along dimension 0
- grad_w_rad: float32 [256, 1536], P(('groups', 'dp')), parts along dimension 0
There are 2 independent parts, one for each index of `groups`. A program takes and returns all parts, laid end to end along the dimension named above; an argument that names none is the same for every part. Nothing has to cross between parts.
Inputs may be any that keep to these rules, and one draw needn't show every extreme that they name: `edge_count`: in every cell exactly one device has all 256 slots live; the others have 256 // 8 to 128 live slots, always its first ones. `edge_source`: the source of an edge slot of device block g is an atom of g's own block or one of the 16 atoms just before or just after it, counted cyclically over the cell's atoms; on every device some edge takes the first and some the last of these atoms. `lattice`: diagonal entries lie in 8 to 10, the others in -1 to 1.
All inputs are finite; a program needn't handle non-finite values.
Results may differ from a plain program's by a relative error of at most 0.014.
Values may be sent and summed in bfloat16 or wider, within the bound.
A program may use at most 64 MiB of HBM per device.

v0:
```python
import math

import jax
import jax.numpy as jnp
from jax import lax
from jax.sharding import PartitionSpec as P

RB = 128
RIM = 16
EDGE_BLOCK = 128


CUTOFF = 48.0
ROOT_THREE = math.sqrt(3.0)
ROOT_FIVE = math.sqrt(5.0)
ROOT_FIFTEEN = math.sqrt(15.0)


def padded_2(cells, sides, width):
    for axis, dim in sides:
        count = lax.axis_size(axis)
        head = lax.slice_in_dim(cells, 0, width, axis=dim)
        tail = lax.slice_in_dim(cells, cells.shape[dim] - width, cells.shape[dim], axis=dim)
        cells = jnp.concatenate(
            [
                lax.ppermute(tail, axis, [(i, (i + 1) % count) for i in range(count)]),
                cells,
                lax.ppermute(head, axis, [((i + 1) % count, i) for i in range(count)]),
            ],
            axis=dim,
        )
    return cells


def geometry(frac_src, frac_tgt, image_shift, lattice_rows, live_mask):
    frac_diff = frac_src + image_shift.astype(jnp.float32) - frac_tgt
    displace = (
        frac_diff[0][None, :] * lattice_rows[0][:, None]
        + frac_diff[1][None, :] * lattice_rows[1][:, None]
        + frac_diff[2][None, :] * lattice_rows[2][:, None]
    )
    distance = jnp.sqrt(jnp.sum(displace * displace, axis=0) + 1.0)
    unit_x = displace[0] / distance
    unit_y = displace[1] / distance
    unit_z = displace[2] / distance
    harm_one = ROOT_THREE * jnp.stack([unit_y, unit_z, unit_x], axis=1)
    harm_two = jnp.stack(
        [
            ROOT_FIFTEEN * unit_x * unit_y,
            ROOT_FIFTEEN * unit_y * unit_z,
            0.5 * ROOT_FIVE * (2.0 * unit_z * unit_z - unit_x * unit_x - unit_y * unit_y),
            ROOT_FIFTEEN * unit_x * unit_z,
            0.5 * ROOT_FIFTEEN * (unit_x * unit_x - unit_y * unit_y),
        ],
        axis=1,
    )
    centres = CUTOFF * jnp.arange(RB, dtype=jnp.float32) / (RB - 1)
    spread = 2.0 * CUTOFF / RB
    envelope = 0.5 * (jnp.cos(math.pi * distance / CUTOFF) + 1.0) * live_mask.astype(jnp.float32)
    radial_basis = (
        jnp.exp(-jnp.square((distance[:, None] - centres[None, :]) / spread)) * envelope[:, None]
    ).astype(jnp.bfloat16)
    return (radial_basis, harm_one, harm_two)


def split_gates(src_rows, radial_gates, harm_one, harm_two):
    channels = src_rows.shape[2]
    src_float = src_rows.astype(jnp.float32)
    scalars = src_float[:, 0, :]
    gate_zero = radial_gates[:, :channels]
    gate_one = radial_gates[:, channels : 2 * channels]
    gate_two = radial_gates[:, 2 * channels :]
    inner_one = harm_one[:, :, None] * scalars[:, None, :] + src_float[:, 1:4, :]
    inner_two = harm_two[:, :, None] * scalars[:, None, :] + src_float[:, 4:9, :]
    return (scalars, gate_zero, gate_one, gate_two, inner_one, inner_two)


def messages(src_rows, radial_gates, harm_one, harm_two):
    scalars, gate_zero, gate_one, gate_two, inner_one, inner_two = split_gates(
        src_rows, radial_gates, harm_one, harm_two
    )
    return jnp.concatenate(
        [
            (gate_zero * scalars)[:, None, :],
            gate_one[:, None, :] * inner_one,
            gate_two[:, None, :] * inner_two,
        ],
        axis=1,
    )


def message_grads(src_rows, radial_gates, harm_one, harm_two, d_msgs):
    scalars, gate_zero, gate_one, gate_two, inner_one, inner_two = split_gates(
        src_rows, radial_gates, harm_one, harm_two
    )
    d_zero = d_msgs[:, 0, :]
    d_one = d_msgs[:, 1:4, :]
    d_two = d_msgs[:, 4:9, :]
    d_gates = jnp.concatenate(
        [d_zero * scalars, jnp.sum(d_one * inner_one, axis=1), jnp.sum(d_two * inner_two, axis=1)],
        axis=1,
    )
    d_scalars = (
        d_zero * gate_zero
        + gate_one * jnp.sum(d_one * harm_one[:, :, None], axis=1)
        + gate_two * jnp.sum(d_two * harm_two[:, :, None], axis=1)
    )
    d_rows = jnp.concatenate(
        [d_scalars[:, None, :], gate_one[:, None, :] * d_one, gate_two[:, None, :] * d_two], axis=1
    )
    return (d_gates, d_rows)


def gated_output(features, summed_b, w_out, cotangent):
    atom_count, comp_count, channels = features.shape
    pre_gate = jnp.dot(
        summed_b.reshape(-1, channels), w_out, preferred_element_type=jnp.float32
    ).reshape(atom_count, comp_count, channels)
    gate_value = jax.nn.sigmoid(pre_gate[:, 0, :])
    new_feats = (features.astype(jnp.float32) + pre_gate * gate_value[:, None, :]).astype(
        jnp.bfloat16
    )
    upstream = cotangent.astype(jnp.float32)
    gate_slope = gate_value * (1.0 - gate_value)
    d_zero = upstream[:, 0, :] * gate_value + gate_slope * jnp.sum(upstream * pre_gate, axis=1)
    d_pregate = jnp.concatenate(
        [d_zero[:, None, :], upstream[:, 1:, :] * gate_value[:, None, :]], axis=1
    ).astype(jnp.bfloat16)
    return (new_feats, d_pregate)


def block_edges(block_id, edge_set, lattice_rows, full_rad):
    tgt_all, src_all, shift_all, live_count, frac_table, frac_target, src_table = edge_set
    first_edge = block_id * EDGE_BLOCK
    tgt_ids = lax.dynamic_slice_in_dim(tgt_all, first_edge, EDGE_BLOCK)
    src_ids = lax.dynamic_slice_in_dim(src_all, first_edge, EDGE_BLOCK)
    image_shift = lax.dynamic_slice_in_dim(shift_all, first_edge, EDGE_BLOCK, 1)
    live_mask = first_edge + jnp.arange(EDGE_BLOCK, dtype=jnp.int32) < live_count
    radial_basis, harm_one, harm_two = geometry(
        frac_table[:, src_ids], frac_target[:, tgt_ids], image_shift, lattice_rows, live_mask
    )
    radial_gates = jnp.dot(radial_basis, full_rad, preferred_element_type=jnp.float32)
    return (tgt_ids, src_ids, radial_basis, harm_one, harm_two, radial_gates, src_table[src_ids])


def forward_sums(edge_set, block_total, lattice_rows, full_rad, start_sum):

    def forward_step(block_id, summed):
        tgt_ids, src_ids, radial_basis, harm_one, harm_two, radial_gates, src_rows = block_edges(
            block_id, edge_set, lattice_rows, full_rad
        )
        return summed.at[tgt_ids].add(messages(src_rows, radial_gates, harm_one, harm_two))

    return lax.fori_loop(0, block_total, forward_step, start_sum)


def backward_sums(edge_set, block_total, lattice_rows, full_rad, d_summed, start_pair):

    def backward_step(block_id, state_pair):
        d_pad, grad_rad = state_pair
        tgt_ids, src_ids, radial_basis, harm_one, harm_two, radial_gates, src_rows = block_edges(
            block_id, edge_set, lattice_rows, full_rad
        )
        d_gates, d_rows = message_grads(
            src_rows, radial_gates, harm_one, harm_two, 0.25 * d_summed[tgt_ids]
        )
        grad_rad = grad_rad + jnp.dot(
            radial_basis.T, d_gates.astype(jnp.bfloat16), preferred_element_type=jnp.float32
        )
        return (d_pad.at[src_ids].add(d_rows), grad_rad)

    return lax.fori_loop(0, block_total, backward_step, start_pair)


def body(
    node_feats,
    frac_pos,
    lattice,
    edge_count,
    edge_target,
    edge_source,
    edge_shift,
    cotangent,
    w_in,
    w_out,
    w_rad,
):
    features = node_feats[0]
    fractions = frac_pos[0]
    lattice_rows = lattice[0]
    live_count = edge_count[0, 0]
    targets = edge_target[0]
    sources = edge_source[0]
    shifts = edge_shift[0]
    upstream = cotangent[0]
    atom_count, comp_count, channels = features.shape
    full_in, full_out, full_rad = (
        lax.all_gather(w_in, "dp", axis=0, tiled=True),
        lax.all_gather(w_out, "dp", axis=0, tiled=True),
        lax.all_gather(w_rad, "dp", axis=0, tiled=True),
    )
    projected = jnp.dot(features.reshape(-1, channels), full_in, preferred_element_type=jnp.float32)
    projected = projected.astype(jnp.bfloat16).reshape(atom_count, comp_count, channels)
    padded = padded_2(projected, (("graph", 0),), RIM)
    frac_pad = padded_2(fractions, (("graph", 1),), RIM)
    rank_count = lax.axis_size("graph")
    first_atom = lax.axis_index("graph") * atom_count
    local_src = jnp.mod(sources - first_atom + RIM, rank_count * atom_count)
    own_set = (targets, local_src, shifts, live_count, frac_pad, fractions, padded)
    own_blocks = (live_count + EDGE_BLOCK - 1) // EDGE_BLOCK
    empty_sum = jnp.zeros((atom_count, comp_count, channels), jnp.float32)
    summed = forward_sums(own_set, own_blocks, lattice_rows, full_rad, empty_sum)
    summed_b = (0.25 * summed).astype(jnp.bfloat16)
    new_feats, d_pregate = gated_output(features, summed_b, full_out, upstream)
    d_summed = jnp.dot(
        d_pregate.reshape(-1, channels), full_out.T, preferred_element_type=jnp.float32
    ).reshape(atom_count, comp_count, channels)
    empty_pad = jnp.zeros((atom_count + 2 * RIM, comp_count, channels), jnp.float32)
    start_pair = (empty_pad, jnp.zeros((RB, 3 * channels), jnp.float32))
    d_pad, grad_rad = backward_sums(
        own_set, own_blocks, lattice_rows, full_rad, d_summed, start_pair
    )
    rim_lo = d_pad[:RIM]
    rim_hi = d_pad[RIM + atom_count :]
    returned = padded_2(
        jnp.concatenate([rim_lo, rim_hi], axis=0).astype(jnp.bfloat16), (("graph", 0),), RIM
    ).astype(jnp.float32)
    own_rows = d_pad[RIM : RIM + atom_count]
    own_rows = own_rows.at[:RIM].add(returned[:RIM])
    own_rows = own_rows.at[atom_count - RIM :].add(returned[3 * RIM :])
    d_proj_b = own_rows.astype(jnp.bfloat16).reshape(-1, channels)
    grad_in = jnp.dot(
        features.reshape(-1, channels).T, d_proj_b, preferred_element_type=jnp.float32
    )
    grad_out = jnp.dot(
        summed_b.reshape(-1, channels).T,
        d_pregate.reshape(-1, channels),
        preferred_element_type=jnp.float32,
    )
    back = jnp.dot(d_proj_b, full_in.T, preferred_element_type=jnp.float32).reshape(
        atom_count, comp_count, channels
    )
    grad_feats = (upstream.astype(jnp.float32) + back).astype(jnp.bfloat16)
    grad_scale = 1.0 / (rank_count * atom_count)
    term_in = grad_scale * grad_in
    term_out = grad_scale * grad_out
    term_rad = grad_scale * grad_rad
    summed_in, summed_out, summed_rad = (
        lax.psum(term_in.astype(jnp.bfloat16), "graph").astype(jnp.float32),
        lax.psum(term_out.astype(jnp.bfloat16), "graph").astype(jnp.float32),
        lax.psum(term_rad.astype(jnp.bfloat16), "graph").astype(jnp.float32),
    )
    grad_w_in, grad_w_out, grad_w_rad = (
        lax.psum_scatter(
            summed_in.astype(jnp.bfloat16), "dp", scatter_dimension=0, tiled=True
        ).astype(jnp.float32),
        lax.psum_scatter(
            summed_out.astype(jnp.bfloat16), "dp", scatter_dimension=0, tiled=True
        ).astype(jnp.float32),
        lax.psum_scatter(
            summed_rad.astype(jnp.bfloat16), "dp", scatter_dimension=0, tiled=True
        ).astype(jnp.float32),
    )
    return (new_feats[None], grad_feats[None], grad_w_in, grad_w_out, grad_w_rad)


def solution(mesh):
    return jax.shard_map(
        body,
        mesh=mesh,
        in_specs=(
            P(("groups", "dp"), "graph", None, None),
            P(("groups", "dp"), None, "graph"),
            P(("groups", "dp"), None, None),
            P(("groups", "dp"), "graph"),
            P(("groups", "dp"), "graph"),
            P(("groups", "dp"), "graph"),
            P(("groups", "dp"), None, "graph"),
            P(("groups", "dp"), "graph", None, None),
            P("dp", None),
            P("dp", None),
            P("dp", None),
        ),
        out_specs=(
            P(("groups", "dp"), "graph", None, None),
            P(("groups", "dp"), "graph", None, None),
            P(("groups", "dp"), None),
            P(("groups", "dp"), None),
            P(("groups", "dp"), None),
        ),
        check_vma=False,
    )
```

profile of v0, /device:TPU:0, one launch (start us, length us, event | category | flops | bytes accessed | tf_op | source)
XLA Modules:
  0.0 381.1 jit_solution(4563539715548942728)
XLA Ops:
  8.6 5.0 %collective-permute-start.1 = (f32[3,16]{1,0:T(4,128)}, f32[3,16]{1,0:T(4,128)S(1)}, u32[]{:S(2)}, u32[]{:S(2)}) collective-permute-start(f32[3,16]{1,0:T(4,128)} %get-tuple-element.553), channel_id=1, source_target_pairs={{4,0},{8,4},{12,8},{0,12},{5,1},{9,5},{13,9},{1,13},{6,2},{10,6},{... | collective-permute-start | bytes 584 | tf_op jit(solution)/shard_map/ppermute | solution.py:28
  15.2 7.3 %all_gather.10 = bf16[512,512]{1,0:T(8,128)(2,1)S(1)} all-gather(bf16[128,512]{1,0:T(8,128)(2,1)S(1)} %copy-done.25), channel_id=1, replica_groups=mesh['groups'=2,'graph'=4,'dp'=4] {'dp'}, dimensions={0}, use_global_device_ids=true | all-gather | bytes 655360 | tf_op jit(solution)/shard_map/all_gather | solution.py:198
  24.0 3.9 %collective-permute-start.3 = (bf16[16,9,512]{2,1,0:T(8,128)(2,1)S(1)}, bf16[16,9,512]{2,1,0:T(8,128)(2,1)S(1)}, u32[]{:S(2)}, u32[]{:S(2)}) collective-permute-start(bf16[16,9,512]{2,1,0:T(8,128)(2,1)S(1)} %slice.298), channel_id=1, source_target_pairs={{4,0},{8,4},{12,8},{0,12},{5,1},{9,5},{13,9},{1,13},{6,2},{10,6},{... | collective-permute-start | bytes 442376 | tf_op jit(solution)/shard_map/ppermute | solution.py:28
  27.8 7.4 %all_gather.11 = bf16[512,512]{1,0:T(8,128)(2,1)} all-gather(bf16[128,512]{1,0:T(8,128)(2,1)S(1)} %copy-done.26), channel_id=1, replica_groups=mesh['groups'=2,'graph'=4,'dp'=4] {'dp'}, dimensions={0}, use_global_device_ids=true | all-gather | bytes 655360 | tf_op jit(solution)/shard_map/all_gather | solution.py:199
  36.9 6.6 %all_gather.9 = bf16[128,1536]{1,0:T(8,128)(2,1)S(1)} all-gather(bf16[32,1536]{1,0:T(8,128)(2,1)S(1)} %copy-done.31), channel_id=1, replica_groups=mesh['groups'=2,'graph'=4,'dp'=4] {'dp'}, dimensions={0}, use_global_device_ids=true | all-gather | bytes 491520 | tf_op jit(solution)/shard_map/all_gather | solution.py:200
  48.3 70.7 %while.28 = (s32[]{:T(128)}, f32[48,9,512]{2,1,0:T(8,128)S(1)}, s32[]{:T(128)}, s32[256]{0:T(256)}, s32[256]{0:T(256)}, /*index=5*/f32[3,80]{0,1:T(8,128)}, s32[...) while((s32[]{:T(128)}, f32[48,9,512]{2,1,0:T(8,128)S(1)}, ...), condition=%wide.region_3.4_spmd, body=%wide.region_0.3_spmd.sunk | while | flops 54439556 | bytes 50134992 | solution.py:154
  49.1 2.0 gather_fusion
  51.1 2.4 copy_convert_fusion.4
  55.5 2.0 gather_fusion.1
  57.5 2.0 gather_fusion.2
  66.7 3.5 copy.77
  70.2 13.5 %scatter_fusion = f32[48,9,512]{2,1,0:T(8,128)S(1)} fusion(f32[48,9,512]{2,1,0:T(8,128)S(1)} %get-tuple-element.851, s32[128]{0:T(128)S(1)} %get-tuple-element.761, f32[128,9,512]{2,1,0:T(8,128)} %copy.77), kind=kCustom, calls=%fused_computation.7.clone.1 | custom fusion | flops 589824 | bytes 7078400 | tf_op jit(solution)/shard_map/while/body/scatter-add | solution.py:152
  84.4 2.0 gather_fusion
  86.5 2.4 copy_convert_fusion.4
  90.8 2.0 gather_fusion.1
  92.8 2.0 gather_fusion.2
  102.0 3.5 copy.77
  105.5 13.5 %scatter_fusion = f32[48,9,512]{2,1,0:T(8,128)S(1)} fusion(f32[48,9,512]{2,1,0:T(8,128)S(1)} %get-tuple-element.851, s32[128]{0:T(128)S(1)} %get-tuple-element.761, f32[128,9,512]{2,1,0:T(8,128)} %copy.77), kind=kCustom, calls=%fused_computation.7.clone.1 | custom fusion | flops 589824 | bytes 7078400 | tf_op jit(solution)/shard_map/while/body/scatter-add | solution.py:152
  125.5 119.3 %while.29 = (s32[]{:T(128)}, f32[80,9,512]{2,1,0:T(8,128)}, f32[128,1536]{1,0:T(8,128)}, s32[]{:T(128)}, s32[256]{0:T(256)}, /*index=5*/s32[256]{0:T(256)}, f32[...) while((s32[]{:T(128)}, f32[80,9,512]{2,1,0:T(8,128)}, ...), condition=%wide.region_12.13_spmd, body=%wide.region_5.12_spmd.sunk | while | flops 109063808 | bytes 48050284 | solution.py:172
  126.3 2.1 gather_fusion.3
  128.4 3.8 copy_convert_fusion.5
  132.2 2.9 gather_fusion.4
  135.1 5.2 %copy_multiply_fusion.2 = f32[128,9,512]{2,0,1:T(8,128)} fusion(f32[128,9,512]{2,1,0:T(8,128)} %gather_fusion.4), kind=kLoop, calls=%fused_computation.60.clone.1 | loop fusion | flops 589824 | bytes 4718592 | tf_op jit(solution)/shard_map/while/body/mul | solution.py:165
  141.8 2.0 gather_fusion.5
  143.8 2.0 gather_fusion.6
  151.8 2.9 fusion.93
  154.6 2.4 fusion.94
  159.1 3.5 copy.80
  162.6 20.1 %scatter_fusion.1 = f32[80,9,512]{2,1,0:T(8,128)} fusion(f32[80,9,512]{2,1,0:T(8,128)} %get-tuple-element.901, s32[128]{0:T(128)S(1)} %get-tuple-element.801, f32[128,9,512]{2,1,0:T(8,128)} %copy.80), kind=kCustom, calls=%fused_computation.8.clone.1 | custom fusion | flops 589824 | bytes 7078400 | tf_op jit(solution)/shard_map/while/body/scatter-add | solution.py:170
  182.7 2.5 convolution_add_fusion.3
  186.0 2.1 gather_fusion.3
  188.0 3.8 copy_convert_fusion.5
  191.9 2.9 gather_fusion.4
  194.7 5.2 %copy_multiply_fusion.2 = f32[128,9,512]{2,0,1:T(8,128)} fusion(f32[128,9,512]{2,1,0:T(8,128)} %gather_fusion.4), kind=kLoop, calls=%fused_computation.60.clone.1 | loop fusion | flops 589824 | bytes 4718592 | tf_op jit(solution)/shard_map/while/body/mul | solution.py:165
  203.4 2.0 gather_fusion.6
  211.4 2.9 fusion.93
  214.3 2.4 fusion.94
  218.7 3.5 copy.80
  222.2 20.1 %scatter_fusion.1 = f32[80,9,512]{2,1,0:T(8,128)} fusion(f32[80,9,512]{2,1,0:T(8,128)} %get-tuple-element.901, s32[128]{0:T(128)S(1)} %get-tuple-element.801, f32[128,9,512]{2,1,0:T(8,128)} %copy.80), kind=kCustom, calls=%fused_computation.8.clone.1 | custom fusion | flops 589824 | bytes 7078400 | tf_op jit(solution)/shard_map/while/body/scatter-add | solution.py:170
  242.4 2.5 convolution_add_fusion.3
  244.8 2.1 convert.25
  247.1 2.0 collective-permute-start.4
  249.2 9.8 %collective-permute-done.5 = bf16[16,9,512]{2,1,0:T(8,128)(2,1)S(1)} collective-permute-done((bf16[16,9,512]{2,1,0:T(8,128)(2,1)S(1)}, bf16[16,9,512]{2,1,0:T(8,128)(2,1)S(1)}, u32[]{:S(2)}, u32[]{:S(2)}) %collective-permute-start.5) | collective-permute-done | bytes 147488 | tf_op jit(solution)/shard_map/ppermute | solution.py:28
  262.8 2.7 fusion.33
  265.5 15.6 %reduce-scatter.10.cloned.1.call-done = bf16[128,512]{1,0:T(8,128)(2,1)} async-done(((bf16[512,512]{1,0:T(8,128)(2,1)}), bf16[128,512]{1,0:T(8,128)(2,1)}) %reduce-scatter.10.cloned.1.call-update) | async-done | bytes 131088
  282.8 22.4 %reduce-scatter.8.cloned.1.call-done = bf16[32,1536]{1,0:T(8,128)(2,1)} async-done(((bf16[128,1536]{1,0:T(8,128)(2,1)}), bf16[32,1536]{1,0:T(8,128)(2,1)}) %reduce-scatter.8.cloned.1.call-update) | async-done | bytes 98320 | tf_op jit(solution)/shard_map/reduce_scatter | solution.py:260
  305.2 24.4 %reduce-scatter.6.cloned.1.call-done = bf16[128,512]{1,0:T(8,128)(2,1)} async-done(((bf16[512,512]{1,0:T(8,128)(2,1)}), bf16[128,512]{1,0:T(8,128)(2,1)}) %reduce-scatter.6.cloned.1.call-update) | async-done | bytes 131088 | tf_op jit(solution)/shard_map/reduce_scatter | solution.py:257
  331.8 37.8 %all-reduce.3.cloned.1.call-done = (bf16[128,512]{0,1:T(8,128)(2,1)}, bf16[128,512]{1,0:T(8,128)(2,1)}, bf16[32,1536]{1,0:T(8,128)(2,1)}) async-done(((bf16[128,512]{0,1:T(8,128)(2,1)}, bf16[128,512]{1,0:T(8,128)(2,1)}, bf16[32,1536]{1,0:T(8,128)(2,1)}), (bf16[128,512]{0,1:T(8,128)(2,1)}, bf16[128,512]{1,0:T(8,128)(2,1)}, bf16[32,1536]{1,0:T(8,128)(2,1)})) %all-reduce.3.cloned.1.call-update) | async-done | bytes 360464 | tf_op jit(solution)/shard_map/psum | solution.py:249
  (251 shorter events, 71.5 us)
Async XLA Ops:
  7.2 8.0 %copy-start.25 = (bf16[128,512]{1,0:T(8,128)(2,1)S(1)}, bf16[128,512]{1,0:T(8,128)(2,1)}, u32[]{:S(2)}) copy-start(bf16[128,512]{1,0:T(8,128)(2,1)} %param.27) | copy-start | bytes 393220
  7.2 274.0 %reduce-scatter.10.cloned.1.call-start = ((), (), s32[]{:S(2)}) async-start(), calls=%async_computation.5 | async-start | bytes 655360
  8.6 38.0 %collective-permute-start.1 = (f32[3,16]{1,0:T(4,128)}, f32[3,16]{1,0:T(4,128)S(1)}, u32[]{:S(2)}, u32[]{:S(2)}) collective-permute-start(f32[3,16]{1,0:T(4,128)} %get-tuple-element.553), channel_id=1, source_target_pairs={{4,0},{8,4},{12,8},{0,12},{5,1},{9,5},{13,9},{1,13},{6,2},{10,6},{... | collective-permute-start | bytes 584 | tf_op jit(solution)/shard_map/ppermute | solution.py:28
  13.6 32.9 %collective-permute-start = (f32[3,16]{1,0:T(4,128)}, f32[3,16]{1,0:T(4,128)}, u32[]{:S(2)}, u32[]{:S(2)}) collective-permute-start(f32[3,16]{1,0:T(4,128)} %get-tuple-element.552), channel_id=1, source_target_pairs={{0,4},{4,8},{8,12},{12,0},{1,5},{5,9},{9,13},{13,1},{2,6},{6,10},{... | collective-permute-start | bytes 584 | tf_op jit(solution)/shard_map/ppermute | solution.py:26
  14.9 12.9 %copy-start.26 = (bf16[128,512]{1,0:T(8,128)(2,1)S(1)}, bf16[128,512]{1,0:T(8,128)(2,1)}, u32[]{:S(2)}) copy-start(bf16[128,512]{1,0:T(8,128)(2,1)} %param.28) | copy-start | bytes 393220
  15.2 21.8 %copy-start.17 = (bf16[432,512]{1,0:T(8,128)(2,1)}, bf16[432,512]{1,0:T(8,128)(2,1)S(1)}, u32[]{:S(2)}) copy-start(bf16[432,512]{1,0:T(8,128)(2,1)S(1)} %reshape_squeeze.4) | copy-start | bytes 1327108
  15.2 20.1 %copy-start.40 = (s32[1,256]{1,0:T(1,128)S(1)}, s32[1,256]{1,0:T(1,128)}, u32[]{:S(2)}) copy-start(s32[1,256]{1,0:T(1,128)} %param.24) | copy-start | bytes 3076
  15.2 20.7 %copy-start.9 = (bf16[1,48,9,512]{3,1,2,0:T(8,128)(2,1)S(1)}, bf16[1,48,9,512]{3,1,2,0:T(8,128)(2,1)}, u32[]{:S(2)}) copy-start(bf16[1,48,9,512]{3,1,2,0:T(8,128)(2,1)} %param.26) | copy-start | bytes 1327108
  23.3 13.6 %copy-start.31 = (bf16[32,1536]{1,0:T(8,128)(2,1)S(1)}, bf16[32,1536]{1,0:T(8,128)(2,1)}, u32[]{:S(2)}) copy-start(bf16[32,1536]{1,0:T(8,128)(2,1)} %param.29) | copy-start | bytes 294916
  23.8 21.2 %copy-start.39 = (s32[1,3,256]{2,0,1:T(1,128)S(1)}, s32[1,3,256]{2,0,1:T(1,128)}, u32[]{:S(2)}) copy-start(s32[1,3,256]{2,0,1:T(1,128)} %param.25) | copy-start | bytes 9220
  23.8 24.2 %collective-permute-start.2 = (bf16[16,9,512]{2,1,0:T(8,128)(2,1)S(1)}, bf16[16,9,512]{2,1,0:T(8,128)(2,1)S(1)}, u32[]{:S(2)}, u32[]{:S(2)}) collective-permute-start(bf16[16,9,512]{2,1,0:T(8,128)(2,1)S(1)} %slice.296), channel_id=1, source_target_pairs={{0,4},{4,8},{8,12},{12,0},{1,5},{5,9},{9,13},{13,1},{2,6},{6,10},{... | collective-permute-start | bytes 442376 | tf_op jit(solution)/shard_map/ppermute | solution.py:26
  24.0 24.1 %collective-permute-start.3 = (bf16[16,9,512]{2,1,0:T(8,128)(2,1)S(1)}, bf16[16,9,512]{2,1,0:T(8,128)(2,1)S(1)}, u32[]{:S(2)}, u32[]{:S(2)}) collective-permute-start(bf16[16,9,512]{2,1,0:T(8,128)(2,1)S(1)} %slice.298), channel_id=1, source_target_pairs={{4,0},{8,4},{12,8},{0,12},{5,1},{9,5},{13,9},{1,13},{6,2},{10,6},{... | collective-permute-start | bytes 442376 | tf_op jit(solution)/shard_map/ppermute | solution.py:28
  53.5 1.4 copy-start.1
  63.8 2.2 copy-start.2
  65.0 1.3 copy-start.32
  88.8 1.4 copy-start.1
  99.1 2.2 copy-start.2
  100.3 1.3 copy-start.32
  119.0 1.6 copy-start.14
  120.2 2.0 copy-start.15
  151.7 2.9 copy-start.35
  151.7 2.9 copy-start.36
  151.7 2.9 copy-start.37
  162.6 20.1 %copy-start.4 = (bf16[128,512]{1,0:T(8,128)(2,1)S(1)}, bf16[128,512]{1,0:T(8,128)(2,1)}, u32[]{:S(2)}) copy-start(bf16[128,512]{1,0:T(8,128)(2,1)} %get-tuple-element.831) | copy-start | bytes 393220 | tf_op jit(solution)/shard_map/while
  162.6 20.1 %copy-start.5 = (bf16[128,512]{1,0:T(8,128)(2,1)S(1)}, bf16[128,512]{1,0:T(8,128)(2,1)}, u32[]{:S(2)}) copy-start(bf16[128,512]{1,0:T(8,128)(2,1)} %get-tuple-element.832) | copy-start | bytes 393220 | tf_op jit(solution)/shard_map/while
  162.6 20.1 %copy-start.28 = (f32[128]{0:T(128)S(1)}, f32[128]{0:T(128)}, u32[]{:S(2)}) copy-start(f32[128]{0:T(128)} %copy-done.27) | copy-start | bytes 1540 | tf_op jit(solution)/shard_map/while
  162.6 20.1 %copy-start.30 = (f32[128]{0:T(128)S(1)}, f32[128]{0:T(128)}, u32[]{:S(2)}) copy-start(f32[128]{0:T(128)} %copy-done.29) | copy-start | bytes 1540 | tf_op jit(solution)/shard_map/while
  211.4 2.9 copy-start.35
  211.4 2.9 copy-start.36
  211.4 2.9 copy-start.37
  222.2 20.1 %copy-start.4 = (bf16[128,512]{1,0:T(8,128)(2,1)S(1)}, bf16[128,512]{1,0:T(8,128)(2,1)}, u32[]{:S(2)}) copy-start(bf16[128,512]{1,0:T(8,128)(2,1)} %get-tuple-element.831) | copy-start | bytes 393220 | tf_op jit(solution)/shard_map/while
  222.2 20.1 %copy-start.5 = (bf16[128,512]{1,0:T(8,128)(2,1)S(1)}, bf16[128,512]{1,0:T(8,128)(2,1)}, u32[]{:S(2)}) copy-start(bf16[128,512]{1,0:T(8,128)(2,1)} %get-tuple-element.832) | copy-start | bytes 393220 | tf_op jit(solution)/shard_map/while
  222.2 20.1 %copy-start.28 = (f32[128]{0:T(128)S(1)}, f32[128]{0:T(128)}, u32[]{:S(2)}) copy-start(f32[128]{0:T(128)} %copy-done.27) | copy-start | bytes 1540 | tf_op jit(solution)/shard_map/while
  222.2 20.1 %copy-start.30 = (f32[128]{0:T(128)S(1)}, f32[128]{0:T(128)}, u32[]{:S(2)}) copy-start(f32[128]{0:T(128)} %copy-done.29) | copy-start | bytes 1540 | tf_op jit(solution)/shard_map/while
  244.8 4.2 %copy-start = (f32[80,9,512]{2,1,0:T(8,128)S(1)}, f32[80,9,512]{2,1,0:T(8,128)}, u32[]{:S(2)}) copy-start(f32[80,9,512]{2,1,0:T(8,128)} %get-tuple-element.361) | copy-start | bytes 4423684
  247.0 12.0 %collective-permute-start.5 = (bf16[16,9,512]{2,1,0:T(8,128)(2,1)S(1)}, bf16[16,9,512]{2,1,0:T(8,128)(2,1)S(1)}, u32[]{:S(2)}, u32[]{:S(2)}) collective-permute-start(bf16[16,9,512]{2,1,0:T(8,128)(2,1)S(1)} %get-tuple-element.547), channel_id=1, source_target_pairs={{4,0},{8,4},{12,8},{0,12},{5,1},{9,5},{13,9},{1,13},{6,2},{10,6},{... | collective-permute-start | bytes 442376 | tf_op jit(solution)/shard_map/ppermute | solution.py:28
  247.1 12.0 %collective-permute-start.4 = (bf16[16,9,512]{2,1,0:T(8,128)(2,1)S(1)}, bf16[16,9,512]{2,1,0:T(8,128)(2,1)S(1)}, u32[]{:S(2)}, u32[]{:S(2)}) collective-permute-start(bf16[16,9,512]{2,1,0:T(8,128)(2,1)S(1)} %get-tuple-element.546), channel_id=1, source_target_pairs={{0,4},{4,8},{8,12},{12,0},{1,5},{5,9},{9,13},{13,1},{2,6},{6,10},{... | collective-permute-start | bytes 442376 | tf_op jit(solution)/shard_map/ppermute | solution.py:26
  259.4 2.4 copy-start.3
  260.3 2.5 copy-start.24
  260.8 2.0 copy-start.20
  261.8 43.5 %reduce-scatter.8.cloned.1.call-start = ((), (), s32[]{:S(2)}) async-start(), calls=%async_computation.4 | async-start | bytes 491520 | tf_op jit(solution)/shard_map/reduce_scatter | solution.py:260
  262.7 67.0 %copy-start.13 = (f32[48,9,512]{2,0,1:T(8,128)S(1)}, f32[48,9,512]{2,0,1:T(8,128)}, u32[]{:S(2)}) copy-start(f32[48,9,512]{2,0,1:T(8,128)} %copy-done.12) | copy-start | bytes 2654212
  262.7 67.0 %copy-start.16 = (bf16[1,48,9,512]{3,1,2,0:T(8,128)(2,1)S(1)}, bf16[1,48,9,512]{3,1,2,0:T(8,128)(2,1)}, u32[]{:S(2)}) copy-start(bf16[1,48,9,512]{3,1,2,0:T(8,128)(2,1)} %param.19) | copy-start | bytes 1327108
  262.7 67.0 %copy-start.22 = (f32[48,512]{1,0:T(8,128)S(1)}, f32[48,512]{1,0:T(8,128)}, u32[]{:S(2)}) copy-start(f32[48,512]{1,0:T(8,128)} %copy-done.21) | copy-start | bytes 294916
  262.7 66.9 %reduce-scatter.6.cloned.1.call-start = ((), (), s32[]{:S(2)}) async-start(), calls=%async_computation.3 | async-start | bytes 655360 | tf_op jit(solution)/shard_map/reduce_scatter | solution.py:257
  265.5 65.1 %copy-start.7 = (bf16[512,512]{1,0:T(8,128)(2,1)S(1)}, bf16[512,512]{1,0:T(8,128)(2,1)}, u32[]{:S(2)}) copy-start(bf16[512,512]{1,0:T(8,128)(2,1)} %copy-done.6) | copy-start | bytes 1572868
  265.5 65.1 %copy-start.11 = (bf16[1,48,9,512]{3,1,2,0:T(8,128)(2,1)S(1)}, bf16[1,48,9,512]{3,1,2,0:T(8,128)(2,1)}, u32[]{:S(2)}) copy-start(bf16[1,48,9,512]{3,1,2,0:T(8,128)(2,1)} %param.26) | copy-start | bytes 1327108
  265.5 104.2 %all-reduce.3.cloned.1.call-start = ((), (), s32[]{:S(2)}) async-start(), calls=%async_computation.6 | async-start | bytes 720896 | tf_op jit(solution)/shard_map/psum | solution.py:249
  (18 other events, 17.0 us)
Sparse Core Ops, SparseCore 0:
  261.9 19.1 reduce-scatter.9
  284.4 20.8 reduce-scatter.7
  307.9 21.6 reduce-scatter.5
  332.6 37.0 all-reduce.2
where the time goes:
time: 385 us; the launch traced here: 381 us
  other arithmetic  137 us (36%)
  waiting for transfers between devices  110 us (29%)
  local copies, waits for them, and re-layouts  73.6 us (19%)
  blocking collectives  21.3 us (6%)
  between operations  14.9 us (4%)
  matrix products  11.9 us (3%)
  starting transfers between devices  11.2 us (3%)
    scatter-add x2, other arithmetic, backward_step(): return (d_pad.at[src_ids].add(d_rows), grad_rad)  40.2 us
    psum x1, waiting for transfers between devices, body(): lax.psum(term_in.astype(jnp.bfloat16), 'graph').astype(jnp.float32)  37.8 us
    scatter-add x2, other arithmetic, forward_step(): summed.at[tgt_ids].add(messages(src_rows, radial_gates, harm_one, harm_two))  27 us
    reduce_scatter x1, waiting for transfers between devices, body(): lax.psum_scatter(summed_out.astype(jnp.bfloat16), 'dp', scatter_dimension...  24.4 us
    reduce_scatter x1, waiting for transfers between devices, body(): lax.psum_scatter(summed_rad.astype(jnp.bfloat16), 'dp', scatter_dimension...  22.4 us
    unnamed x5, waiting for transfers between devices  15.7 us
    convert_element_type x4, other arithmetic, split_gates(): src_float = src_rows.astype(jnp.float32)  12.3 us
    unnamed x61, local copies, waits for them, and re-layouts  11.3 us
  transfers between devices with their start and end apart: 10, of which 5 were waited for; matrix products, arithmetic and copies ran while one was open for 4% of the time, Pallas kernels for 0%

commit v1 on v0

v1 whole, which is shorter than its diff:
```python
import functools
import math

import jax
import jax.numpy as jnp
from jax import lax
from jax.experimental import pallas as pl
from jax.experimental.pallas import tpu as pltpu
from jax.sharding import PartitionSpec as P

RB = 128
RIM = 16
EDGE_ROWS = 16
CUTOFF = 48.0
ROOT_THREE = math.sqrt(3.0)
ROOT_FIVE = math.sqrt(5.0)
ROOT_FIFTEEN = math.sqrt(15.0)
MESH = pl.DeviceIdType.MESH
F32 = jnp.float32
BF16 = jnp.bfloat16


def dot(a, b, dims=((1,), (0,))):
    return lax.dot_general(a, b, (dims, ((), ())), preferred_element_type=F32)


def log2(value):
    bits = value.bit_length() - 1
    assert 1 << bits == value
    return bits


class Reduction:
    def __init__(self, place, bufs, sems, out_ref):
        self.place = place
        self.part, self.ra, self.sb, self.rb, self.sc, self.rc, self.rd = bufs
        self.a_s, self.a_r, self.b_s, self.b_r, self.c_s, self.c_r, self.d_s, self.d_r = sems
        self.out_ref = out_ref
        self.sends = []
        self.split = self.rd.shape[1] != self.out_ref.shape[0]

    def send(self, src, dst, send_sem, recv_sem, where):
        copy = pltpu.make_async_remote_copy(
            src_ref=src, dst_ref=dst, send_sem=send_sem, recv_sem=recv_sem,
            device_id=where, device_id_type=MESH,
        )
        copy.start()
        self.sends.append(copy)

    def arrived(self, dst, send_sem, recv_sem, where):
        pltpu.make_async_remote_copy(
            src_ref=dst, dst_ref=dst, send_sem=send_sem, recv_sem=recv_sem,
            device_id=where, device_id_type=MESH,
        ).wait_recv()

    def put(self, value):
        x_count, n = self.part.shape[1], self.part.shape[2]
        for r in range(2 * x_count):
            self.part[r % 2, r // 2] = value[r * n : (r + 1) * n].astype(BF16)

    def stage_a(self):
        core, peer = self.place["core"], self.place["peer"]
        self.send(self.part.at[1 - core], self.ra, self.a_s, self.a_r, {"dp": peer})

    def stage_b(self):
        core, peer, x, xs = (self.place[k] for k in ("core", "peer", "x", "x_count"))
        self.arrived(self.ra, self.a_s, self.a_r, {"dp": peer})
        for i in range(xs):
            self.sb[i] = (self.part.at[core, i][...].astype(F32) + self.ra[i].astype(F32)).astype(BF16)
        for j in range(1, xs):
            to = lax.rem(x + j, xs)
            self.send(self.sb.at[to], self.rb.at[x], self.b_s.at[j], self.b_r.at[x], {"dp": 2 * to + core})

    def stage_c(self):
        core, x, xs, z, zs = (self.place[k] for k in ("core", "x", "x_count", "z", "z_count"))
        total = self.sb.at[x][...].astype(F32)
        for j in range(1, xs):
            frm = lax.rem(x + xs - j, xs)
            self.arrived(self.rb.at[frm], self.b_s.at[j], self.b_r.at[frm], {"dp": 2 * frm + core})
            total = total + self.rb.at[frm][...].astype(F32)
        if self.split:
            self.sc[...] = total.astype(BF16).reshape(self.sc.shape)
            for j in range(1, zs):
                to = lax.rem(z + j, zs)
                self.send(self.sc.at[to], self.rc.at[z], self.c_s.at[j], self.c_r.at[z], {"graph": to})
        else:
            self.rd.at[z][...] = total.astype(BF16)
            self.spread()

    def spread(self):
        z, zs = self.place["z"], self.place["z_count"]
        for j in range(1, zs):
            to = lax.rem(z + j, zs)
            self.send(self.rd.at[z], self.rd.at[z], self.d_s.at[j], self.d_r.at[z], {"graph": to})

    def stage_d(self):
        z, zs = self.place["z"], self.place["z_count"]
        if self.split:
            total = self.sc.at[z][...].astype(F32)
            for j in range(1, zs):
                frm = lax.rem(z + zs - j, zs)
                self.arrived(self.rc.at[frm], self.c_s.at[j], self.c_r.at[frm], {"graph": frm})
                total = total + self.rc.at[frm][...].astype(F32)
            self.rd.at[z][...] = total.astype(BF16)
            self.spread()

    def finish(self):
        z, zs = self.place["z"], self.place["z_count"]
        for j in range(1, zs):
            frm = lax.rem(z + zs - j, zs)
            self.arrived(self.rd.at[frm], self.d_s.at[j], self.d_r.at[frm], {"graph": frm})
        if self.split:
            self.out_ref[...] = self.rd[...].reshape(self.out_ref.shape)
        else:
            total = self.rd[0].astype(F32)
            for i in range(1, zs):
                total = total + self.rd[i].astype(F32)
            self.out_ref[...] = total.astype(BF16)


def kernel(
    x_count, z_count,
    feat_ref, cot_ref, geo_ref, frac_ref, win_ref, wout_ref, wrad_ref,
    new_ref, gf_ref, gin_ref, gout_ref, grad_ref,
    full_in, full_out, full_rad, feat_pad, frac_pad, proj, rows_e, msg_e, dmsg_e, gates, dgates,
    table, columns, basis_l, basis_r, pre, summed_s, dpre_s, dsum_s, d_pad, rim_lo, rim_hi, dproj_s,
    w_send, w_recv, h_send, h_recv, *red_scratch,
):
    comps, atoms, channels = feat_ref.shape
    edges = geo_ref.shape[1]
    padded = atoms + 2 * RIM
    z = lax.axis_index("graph")
    d = lax.axis_index("dp")
    x, core = lax.div(d, 2), lax.rem(d, 2)
    peer = 2 * x + 1 - core
    place = dict(core=core, peer=peer, x=x, x_count=x_count, z=z, z_count=z_count)
    sends = []

    barrier = pltpu.get_barrier_semaphore()
    for j in range(1, z_count):
        pl.semaphore_signal(barrier, inc=1, device_id={"graph": lax.rem(z + j, z_count)}, device_id_type=MESH)
    for j in range(1, x_count):
        pl.semaphore_signal(
            barrier, inc=1, device_id={"dp": 2 * lax.rem(x + j, x_count) + core}, device_id_type=MESH
        )
    pl.semaphore_signal(barrier, inc=1, device_id={"dp": peer}, device_id_type=MESH)
    pl.semaphore_wait(barrier, z_count - 1 + x_count)

    def remote(src, dst, send_sem, recv_sem, where):
        return pltpu.make_async_remote_copy(
            src_ref=src, dst_ref=dst, send_sem=send_sem, recv_sem=recv_sem,
            device_id=where, device_id_type=MESH,
        )

    def send(*args):
        copy = remote(*args)
        copy.start()
        sends.append(copy)

    def gather_start(i, w_ref, full):
        for j in range(1, x_count):
            to = 2 * lax.rem(x + j, x_count) + core
            send(w_ref, full.at[d], w_send.at[i, j], w_recv.at[i, d], {"dp": to})
        send(w_ref, full.at[d], w_send.at[i, 0], w_recv.at[i, d], {"dp": peer})
        full.at[d][...] = w_ref[...]

    def gather_forward(i, full):
        for j in range(1, x_count):
            frm = 2 * lax.rem(x + x_count - j, x_count) + core
            remote(full.at[frm], full.at[frm], w_send.at[i, j], w_recv.at[i, frm], {"dp": frm}).wait_recv()
            send(full.at[frm], full.at[frm], w_send.at[i, x_count + j - 1], w_recv.at[i, frm], {"dp": peer})

    def gather_finish(i, full):
        for j in range(x_count):
            frm = 2 * lax.rem(x + x_count - j, x_count) + 1 - core
            remote(full.at[frm], full.at[frm], w_send.at[i, 0], w_recv.at[i, frm], {"dp": peer}).wait_recv()

    right = {"graph": lax.rem(z + 1, z_count)}
    left = {"graph": lax.rem(z + z_count - 1, z_count)}
    last = atoms - RIM
    ahead = RIM + atoms
    send(frac_ref.at[last:atoms], frac_pad.at[0:RIM], h_send.at[0], h_recv.at[0], right)
    send(frac_ref.at[0:RIM], frac_pad.at[ahead:padded], h_send.at[1], h_recv.at[1], left)
    gather_start(0, win_ref, full_in)
    send(feat_ref.at[:, last:atoms], feat_pad.at[:, 0:RIM], h_send.at[2], h_recv.at[2], right)
    send(feat_ref.at[:, 0:RIM], feat_pad.at[:, ahead:padded], h_send.at[3], h_recv.at[3], left)
    gather_start(1, wrad_ref, full_rad)

    feat_pad[:, RIM:ahead, :] = feat_ref[...]
    frac_pad[RIM:ahead, :] = frac_ref[...]
    remote(frac_pad.at[0:RIM], frac_pad.at[0:RIM], h_send.at[0], h_recv.at[0], left).wait_recv()
    remote(frac_pad.at[ahead:padded], frac_pad.at[ahead:padded], h_send.at[1], h_recv.at[1], right).wait_recv()

    tgt_row = geo_ref[13:14, :]
    src_row = geo_ref[14:15, :]
    hot_src_t = lax.broadcasted_iota(jnp.int32, (padded, edges), 0).astype(F32) == src_row
    hot_tgt_t = lax.broadcasted_iota(jnp.int32, (atoms, edges), 0).astype(F32) == tgt_row
    diffs = []
    for i in range(3):
        f_src = jnp.sum(jnp.where(hot_src_t, frac_pad[:, i : i + 1], 0.0), axis=0, keepdims=True)
        f_tgt = jnp.sum(jnp.where(hot_tgt_t, frac_ref[:, i : i + 1], 0.0), axis=0, keepdims=True)
        diffs.append(f_src + geo_ref[i : i + 1, :] - f_tgt)
    displace = [
        sum(diffs[i] * geo_ref[3 + 3 * i + j : 4 + 3 * i + j, :] for i in range(3)) for j in range(3)
    ]
    distance = jnp.sqrt(
        displace[0] * displace[0] + displace[1] * displace[1] + displace[2] * displace[2] + 1.0
    )
    ux, uy, uz = (displace[j] / distance for j in range(3))
    envelope = 0.5 * (jnp.cos(math.pi * distance / CUTOFF) + 1.0) * geo_ref[12:13, :]
    table[...] = jnp.zeros_like(table)
    entries = [
        envelope,
        ROOT_THREE * uy,
        ROOT_THREE * uz,
        ROOT_THREE * ux,
        ROOT_FIFTEEN * ux * uy,
        ROOT_FIFTEEN * uy * uz,
        0.5 * ROOT_FIVE * (2.0 * uz * uz - ux * ux - uy * uy),
        ROOT_FIFTEEN * ux * uz,
        0.5 * ROOT_FIFTEEN * (ux * ux - uy * uy),
        distance,
        tgt_row,
        src_row,
    ]
    for i, entry in enumerate(entries):
        table[i : i + 1, :] = entry
    columns[...] = table[...].T
    hot_src = (
        lax.broadcasted_iota(jnp.int32, (edges, padded), 1).astype(F32) == columns[:, 11:12]
    ).astype(BF16)
    hot_tgt = (
        lax.broadcasted_iota(jnp.int32, (edges, atoms), 1).astype(F32) == columns[:, 10:11]
    ).astype(BF16)
    hot_src_t = hot_src_t.astype(BF16)
    hot_tgt_t = hot_tgt_t.astype(BF16)

    ranks, rad_rows, rad_cols = full_rad.shape
    quarter = rad_rows // 2
    slot = lax.broadcasted_iota(jnp.int32, (1, 2 * RB), 1)
    half = (slot >> log2(quarter)) & 1
    index = ((slot >> log2(rad_rows)) << log2(quarter)) + (slot & (quarter - 1))
    centres = CUTOFF * index.astype(F32) / (RB - 1)
    offset = (columns[:, 9:10] - centres) / (2.0 * CUTOFF / RB)
    basis = jnp.exp(-(offset * offset)) * columns[:, 0:1]
    basis_l[...] = jnp.where(half == 0, basis, 0.0).astype(BF16)
    basis_r[...] = jnp.where(half == 1, basis, 0.0).astype(BF16)

    gather_forward(0, full_in)
    gather_start(2, wout_ref, full_out)
    gather_forward(1, full_rad)
    gather_finish(0, full_in)
    remote(feat_pad.at[:, 0:RIM], feat_pad.at[:, 0:RIM], h_send.at[2], h_recv.at[2], left).wait_recv()
    remote(feat_pad.at[:, ahead:padded], feat_pad.at[:, ahead:padded], h_send.at[3], h_recv.at[3], right).wait_recv()
    proj[...] = (
        dot(feat_pad[...].reshape(comps * padded, channels), full_in[...].reshape(channels, channels))
        .astype(BF16)
        .reshape(comps, padded, channels)
    )
    for k in range(comps):
        rows_e[k] = dot(hot_src, proj[k]).astype(BF16)
    gather_finish(1, full_rad)
    rad = full_rad[...].reshape(ranks * rad_rows, rad_cols)
    gates[:, :rad_cols] = dot(basis_l[...], rad)
    gates[:, rad_cols:] = dot(basis_r[...], rad)
    gather_forward(2, full_out)

    def gate_of(rows):
        return [gates[rows, i * channels : (i + 1) * channels] for i in range(3)]

    @pl.loop(0, edges // EDGE_ROWS)
    def _(step):
        rows = pl.ds(pl.multiple_of(step * EDGE_ROWS, EDGE_ROWS), EDGE_ROWS)
        harm = columns[rows, :]
        g0, g1, g2 = gate_of(rows)
        scalars = rows_e[0, rows, :].astype(F32)
        msg_e[0, rows, :] = (g0 * scalars).astype(BF16)
        for k in range(1, comps):
            inner = harm[:, k : k + 1] * scalars + rows_e[k, rows, :].astype(F32)
            msg_e[k, rows, :] = ((g1 if k < 4 else g2) * inner).astype(BF16)

    for k in range(comps):
        summed_s[k] = (0.25 * dot(hot_tgt_t, msg_e[k])).astype(BF16)
    gather_finish(2, full_out)
    w_out = full_out[...].reshape(channels, channels)
    flat = (comps * atoms, channels)
    pre[...] = dot(summed_s[...].reshape(flat), w_out).reshape(comps, atoms, channels)

    @pl.loop(0, atoms // 16)
    def _(step):
        rows = pl.ds(pl.multiple_of(step * 16, 16), 16)
        p0 = pre[0, rows, :]
        gate = jax.nn.sigmoid(p0)
        total = jnp.zeros_like(gate)
        for k in range(comps):
            p = pre[k, rows, :]
            u = cot_ref[k, rows, :].astype(F32)
            total = total + u * p
            new_ref[k, rows, :] = (feat_ref[k, rows, :].astype(F32) + p * gate).astype(BF16)
            if k:
                dpre_s[k, rows, :] = (u * gate).astype(BF16)
        u0 = cot_ref[0, rows, :].astype(F32)
        dpre_s[0, rows, :] = (u0 * gate + gate * (1.0 - gate) * total).astype(BF16)

    scale = 1.0 / (z_count * atoms)
    count = len(red_scratch) // 3
    reds = [
        Reduction(place, red_scratch[i * count : i * count + 7], red_scratch[i * count + 7 : (i + 1) * count], out)
        for i, out in enumerate((gout_ref, grad_ref, gin_ref))
    ]
    red_out, red_rad, red_in = reds
    across = ((0,), (0,))
    red_out.put(scale * dot(summed_s[...].reshape(flat), dpre_s[...].reshape(flat), across))
    red_out.stage_a()
    dsum_s[...] = (
        (0.25 * dot(dpre_s[...].reshape(flat), w_out, ((1,), (1,)))).astype(BF16).reshape(comps, atoms, channels)
    )
    red_out.stage_b()
    for k in range(comps):
        dmsg_e[k] = dot(hot_tgt, dsum_s[k]).astype(BF16)

    @pl.loop(0, edges // EDGE_ROWS)
    def _(step):
        rows = pl.ds(pl.multiple_of(step * EDGE_ROWS, EDGE_ROWS), EDGE_ROWS)
        harm = columns[rows, :]
        g0, g1, g2 = gate_of(rows)
        scalars = rows_e[0, rows, :].astype(F32)
        d0 = dmsg_e[0, rows, :].astype(F32)
        dgates[rows, 0:channels] = (d0 * scalars).astype(BF16)
        d_scalars = d0 * g0
        for lo, hi, gate in ((1, 4, g1), (4, 9, g2)):
            mixed = jnp.zeros_like(d0)
            plain = jnp.zeros_like(d0)
            for k in range(lo, hi):
                dk = dmsg_e[k, rows, :].astype(F32)
                mixed = mixed + dk * harm[:, k : k + 1]
                plain = plain + dk * rows_e[k, rows, :].astype(F32)
                msg_e[k, rows, :] = (gate * dk).astype(BF16)
            block = 1 if lo == 1 else 2
            dgates[rows, block * channels : (block + 1) * channels] = (mixed * scalars + plain).astype(BF16)
            d_scalars = d_scalars + gate * mixed
        msg_e[0, rows, :] = d_scalars.astype(BF16)

    red_out.stage_c()
    for k in range(comps):
        d_pad[k] = dot(hot_src_t, msg_e[k]).astype(BF16)
    red_in.put(
        scale
        * dot(
            feat_pad[...].reshape(comps * padded, channels),
            d_pad[...].reshape(comps * padded, channels),
            across,
        )
    )
    red_in.stage_a()
    send(d_pad.at[:, 0:RIM], rim_hi, h_send.at[4], h_recv.at[4], left)
    send(d_pad.at[:, ahead:padded], rim_lo, h_send.at[5], h_recv.at[5], right)
    red_rad.put(
        scale
        * (
            dot(basis_l[...], dgates[:, :rad_cols], across)
            + dot(basis_r[...], dgates[:, rad_cols:], across)
        )
    )
    red_rad.stage_a()
    red_in.stage_b()
    red_rad.stage_b()
    red_out.stage_d()
    red_in.stage_c()
    red_rad.stage_c()
    remote(rim_hi, rim_hi, h_send.at[4], h_recv.at[4], right).wait_recv()
    remote(rim_lo, rim_lo, h_send.at[5], h_recv.at[5], left).wait_recv()
    dproj_s[...] = d_pad[:, RIM:ahead, :]
    dproj_s[:, 0:RIM, :] = (dproj_s[:, 0:RIM, :].astype(F32) + rim_lo[...].astype(F32)).astype(BF16)
    dproj_s[:, last:atoms, :] = (dproj_s[:, last:atoms, :].astype(F32) + rim_hi[...].astype(F32)).astype(BF16)
    red_in.stage_d()
    red_rad.stage_d()
    back = dot(dproj_s[...].reshape(flat), full_in[...].reshape(channels, channels), ((1,), (1,)))
    gf_ref[...] = (
        (cot_ref[...].reshape(flat).astype(F32) + back).astype(BF16).reshape(comps, atoms, channels)
    )
    for red in reds:
        red.finish()
    for red in reds:
        for copy in red.sends:
            copy.wait_send()
    for copy in sends:
        copy.wait_send()


def body(x_count, z_count, node_feats, frac_pos, lattice, edge_count, edge_target, edge_source,
         edge_shift, cotangent, w_in, w_out, w_rad):
    atoms, comps, channels = node_feats.shape[1:]
    edges = edge_target.shape[1]
    padded = atoms + 2 * RIM
    dp = 2 * x_count
    feats = jnp.transpose(node_feats[0], (1, 0, 2))
    cot = jnp.transpose(cotangent[0], (1, 0, 2))
    frac = jnp.pad(frac_pos[0].T, ((0, 0), (0, 125)))
    first = lax.axis_index("graph") * atoms
    local_src = jnp.mod(edge_source[0] - first + RIM, z_count * atoms)
    live = jnp.arange(edges, dtype=jnp.int32) < edge_count[0, 0]
    geo = jnp.concatenate(
        [
            edge_shift[0].astype(F32),
            jnp.broadcast_to(lattice[0].reshape(9, 1), (9, edges)),
            live.astype(F32)[None],
            edge_target[0].astype(F32)[None],
            local_src.astype(F32)[None],
            jnp.zeros((1, edges), F32),
        ],
        axis=0,
    )
    rad_cols = w_rad.shape[1] // 2
    rad = jnp.concatenate([w_rad[:, :rad_cols], w_rad[:, rad_cols:]], axis=0)
    rows, rad_rows = w_in.shape[0], rad.shape[0]

    vmem = lambda shape, dtype=BF16: pltpu.VMEM(shape, dtype)
    dma = pltpu.SemaphoreType.DMA
    scratch = [
        vmem((dp, rows, channels)), vmem((dp, rows, channels)), vmem((dp, rad_rows, rad_cols)),
        vmem((comps, padded, channels)), vmem((padded, 128), F32), vmem((comps, padded, channels)),
        vmem((comps, edges, channels)), vmem((comps, edges, channels)), vmem((comps, edges, channels)),
        vmem((edges, 3 * channels), F32), vmem((edges, 3 * channels)),
        vmem((128, edges), F32), vmem((edges, 128), F32), vmem((edges, 2 * RB)), vmem((edges, 2 * RB)),
        vmem((comps, atoms, channels), F32), vmem((comps, atoms, channels)),
        vmem((comps, atoms, channels)), vmem((comps, atoms, channels)),
        vmem((comps, padded, channels)), vmem((comps, RIM, channels)), vmem((comps, RIM, channels)),
        vmem((comps, atoms, channels)),
        dma((3, 2 * x_count)), dma((3, dp)), dma((6,)), dma((6,)),
    ]
    for n, cols in ((rows, channels), (rad_rows, rad_cols), (rows, channels)):
        piece = n // z_count if n % (16 * z_count) == 0 else n
        scratch += [
            vmem((2, x_count, n, cols)), vmem((x_count, n, cols)), vmem((x_count, n, cols)),
            vmem((x_count, n, cols)), vmem((n // piece, piece, cols)), vmem((z_count, piece, cols)),
            vmem((z_count, piece, cols)),
            dma, dma, dma((x_count,)), dma((x_count,)), dma((z_count,)), dma((z_count,)),
            dma((z_count,)), dma((z_count,)),
        ]
    whole = pl.BlockSpec(memory_space=pltpu.VMEM)
    new, grad_feats, g_in, g_out, g_rad = pl.pallas_call(
        functools.partial(kernel, x_count, z_count),
        out_shape=[
            jax.ShapeDtypeStruct((comps, atoms, channels), BF16),
            jax.ShapeDtypeStruct((comps, atoms, channels), BF16),
            jax.ShapeDtypeStruct((rows, channels), BF16),
            jax.ShapeDtypeStruct((rows, channels), BF16),
            jax.ShapeDtypeStruct((rad_rows, rad_cols), BF16),
        ],
        in_specs=[whole] * 7,
        out_specs=[whole] * 5,
        scratch_shapes=scratch,
        compiler_params=pltpu.CompilerParams(
            collective_id=0, has_side_effects=True, vmem_limit_bytes=50 * 1024 * 1024
        ),
    )(feats, cot, geo, frac, w_in, w_out, rad)
    g_rad = g_rad.astype(F32)
    half = rad_rows // 2
    return (
        jnp.transpose(new, (1, 0, 2))[None],
        jnp.transpose(grad_feats, (1, 0, 2))[None],
        g_in.astype(F32),
        g_out.astype(F32),
        jnp.concatenate([g_rad[:half], g_rad[half:]], axis=1),
    )


def solution(mesh):
    return jax.shard_map(
        functools.partial(body, mesh.shape["dp"] // 2, mesh.shape["graph"]),
        mesh=mesh,
        in_specs=(
            P(("groups", "dp"), "graph", None, None),
            P(("groups", "dp"), None, "graph"),
            P(("groups", "dp"), None, None),
            P(("groups", "dp"), "graph"),
            P(("groups", "dp"), "graph"),
            P(("groups", "dp"), "graph"),
            P(("groups", "dp"), None, "graph"),
            P(("groups", "dp"), "graph", None, None),
            P("dp", None),
            P("dp", None),
            P("dp", None),
        ),
        out_specs=(
            P(("groups", "dp"), "graph", None, None),
            P(("groups", "dp"), "graph", None, None),
            P(("groups", "dp"), None),
            P(("groups", "dp"), None),
            P(("groups", "dp"), None),
        ),
        check_vma=False,
    )
```

time: 385 us -> 60.9 us (0.16)
  other arithmetic: 137 us -> 4.93 us
  waiting for transfers between devices: 110 us -> 0 us
  local copies, waits for them, and re-layouts: 73.6 us -> 5.43 us
  Pallas kernels: 0 us -> 48.8 us
  blocking collectives: 21.3 us -> 0 us
  between operations: 14.9 us -> 1.42 us
  matrix products: 11.9 us -> 0 us
  starting transfers between devices: 11.2 us -> 0 us
    scatter-add x6 -> x0, other arithmetic: 67.4 us -> none  [the longest x2 40.2 us: backward_step(): return (d_pad.at[src_ids].add(d_rows), grad_rad)]
    pallas_call x0 -> x1, Pallas kernels: none -> 48.8 us  [body(): pl.pallas_call(functools.partial(kernel, x_count, z_count), out_shape=[ja...]
    reduce_scatter x2 -> x0, waiting for transfers between devices: 46.8 us -> none  [the longest x1 24.4 us: body(): lax.psum_scatter(summed_out.astype(jnp.bfloat16), 'dp', scatter_dimension...]
    psum x1 -> x0, waiting for transfers between devices: 37.8 us -> none  [body(): lax.psum(term_in.astype(jnp.bfloat16), 'graph').astype(jnp.float32)]
    gather x14 -> x0, local copies, waits for them, and re-layouts: 29.9 us -> none  [the longest x4 8.18 us: block_edges(): src_table[src_ids]]
    all_gather x3 -> x0, blocking collectives: 21.3 us -> none  [the longest x1 7.45 us: body(): lax.all_gather(w_out, 'dp', axis=0, tiled=True)]
    mul x22 -> x0, other arithmetic: 18 us -> none  [the longest x2 10.4 us: backward_step(): 0.25 * d_summed[tgt_ids]]
    unnamed x5 -> x0, waiting for transfers between devices: 15.7 us -> none
  transfers between devices with their start and end apart: 10 -> 0, of which waited for: 5 -> 0; matrix products, arithmetic and copies ran while one was open for 4% -> 0% of each run, Pallas kernels for 0% -> 0%
where the time goes in v1:
time: 60.9 us; the launch traced here: 60.6 us
  Pallas kernels  48.8 us (80%)
  local copies, waits for them, and re-layouts  5.43 us (9%)
  other arithmetic  4.93 us (8%)
  between operations  1.42 us (2%)
    pallas_call x1, Pallas kernels, body(): pl.pallas_call(functools.partial(kernel, x_count, z_count), out_shape=[ja...  48.8 us
    unnamed x13, local copies, waits for them, and re-layouts  5.11 us

profile of v1, /device:TPU:0, one launch (start us, length us, event | category | flops | bytes accessed | tf_op | source)
XLA Modules:
  0.0 60.6 jit_solution(17130343722102095651)
XLA Ops:
  0.6 0.0 copy-start.4
  0.6 0.0 copy-start
  1.4 0.7 %fusion.1 = f32[1,256]{1,0:T(1,128)S(1)} fusion(s32[1,256]{1,0:T(1,128)} %param.16, s32[]{:T(128)S(6)} %mul.3), kind=kLoop, calls=%fused_computation.6 | loop fusion | flops 2304 | bytes 2052 | tf_op jit(solution)/shard_map/convert_element_type | solution.py:409
  2.1 0.7 %convert_element_type.38 = f32[1,256]{1,0:T(1,128)S(1)} convert(s32[1,256]{1,0:T(1,128)} %param.15) | non-fusion elementwise | flops 256 | bytes 2048 | tf_op jit(solution)/shard_map/convert_element_type | solution.py:408
  2.8 0.7 %reduce = f32[3,3]{1,0:T(4,128)S(1)} reduce(f32[1,3,3]{2,0,1:T(1,128)} %param.13, f32[]{:T(128)} %constant.35), dimensions={0}, to_apply=%param.13.reduce_sub_computation | reduce | bytes 76 | tf_op args[2]
  3.5 0.1 broadcast_in_dim.19
  3.5 0.7 %fusion = f32[3,256]{1,0:T(4,128)S(1)} fusion(s32[1,3,256]{2,0,1:T(1,128)} %param.17), kind=kLoop, calls=%fused_computation.3 | loop fusion | flops 768 | bytes 6144 | tf_op jit(solution)/shard_map/convert_element_type | solution.py:405
  4.2 0.1 broadcast_in_dim.20
  4.3 0.1 concatenate.9.geo_ref
  4.4 0.8 %copy.17 = f32[1,3,48]{1,2,0:T(8,128)S(1)} copy(f32[1,3,48]{2,0,1:T(1,128)} %param.12) | data formatting | bytes 1152 | tf_op args[1]
  5.2 0.0 copy-done.4
  5.2 0.0 copy-done
  5.3 0.0 copy-start.1
  5.3 1.0 %copy-done.1 = bf16[1,48,9,512]{3,1,2,0:T(8,128)(2,1)S(1)} copy-done((bf16[1,48,9,512]{3,1,2,0:T(8,128)(2,1)S(1)}, bf16[1,48,9,512]{3,1,2,0:T(8,128)(2,1)}, u32[]{:S(2)}) %copy-start.1) | copy-done | bytes 442392
  6.3 0.0 copy-start.2
  6.3 0.9 %copy-done.2 = bf16[128,512]{1,0:T(8,128)(2,1)S(1)} copy-done((bf16[128,512]{1,0:T(8,128)(2,1)S(1)}, bf16[128,512]{1,0:T(8,128)(2,1)}, u32[]{:S(2)}) %copy-start.2) | copy-done | bytes 131096
  7.2 0.0 copy-start.3
  7.2 0.9 %copy-done.3 = bf16[128,512]{1,0:T(8,128)(2,1)S(1)} copy-done((bf16[128,512]{1,0:T(8,128)(2,1)S(1)}, bf16[128,512]{1,0:T(8,128)(2,1)}, u32[]{:S(2)}) %copy-start.3) | copy-done | bytes 131096
  8.1 48.8 %shard_map.146 = (bf16[9,48,512]{2,1,0:T(8,128)(2,1)S(1)}, bf16[9,48,512]{2,1,0:T(8,128)(2,1)S(1)}, bf16[128,512]{1,0:T(8,128)(2,1)S(1)}, bf16[128,512]{1,0:T(8,128)(2,1)S(1)}, bf16[64,768]{1,0:T(8,128)(2,1)S(1)}) custom-call(bf16[9,48,512]{2,1,0:T(8,128)(2,1)S(1)} %bitcast.19, bf16[9,48,512]{2,1,0:T(8,128)(2,1)S(1)} %bitcast.20, ...), custom_call_target="tpu_custom_call" | custom-call | tf_op jit(solution)/shard_map/pallas_call | solution.py:442
  56.9 0.7 %pad_maximum_fusion = f32[32,1536]{1,0:T(8,128)} fusion(f32[32,768]{1,0:T(8,128)S(1)} %get-tuple-element.16, f32[32,768]{1,0:T(8,128)S(1)} %get-tuple-element.15), kind=kLoop, calls=%fused_computation | loop fusion | flops 49152 | bytes 393216 | tf_op jit(solution)/shard_map/concatenate | solution.py:465
  57.6 0.7 %convert_element_type.40 = f32[128,512]{1,0:T(8,128)} convert(bf16[128,512]{1,0:T(8,128)(2,1)S(1)} %get-tuple-element.12) | non-fusion elementwise | flops 65536 | bytes 393216 | tf_op jit(solution)/shard_map/convert_element_type | solution.py:463
  58.3 0.7 %convert_element_type.41 = f32[128,512]{1,0:T(8,128)} convert(bf16[128,512]{1,0:T(8,128)(2,1)S(1)} %get-tuple-element.13) | non-fusion elementwise | flops 65536 | bytes 393216 | tf_op jit(solution)/shard_map/convert_element_type | solution.py:464
  59.1 0.8 %copy.24 = bf16[1,48,9,512]{3,1,2,0:T(8,128)(2,1)} copy(bf16[1,48,9,512]{3,1,2,0:T(8,128)(2,1)S(1)} %bitcast.22) | data formatting | bytes 884736
  59.8 0.8 %copy.25 = bf16[1,48,9,512]{3,1,2,0:T(8,128)(2,1)} copy(bf16[1,48,9,512]{3,1,2,0:T(8,128)(2,1)S(1)} %bitcast.21) | data formatting | bytes 884736
  (6 shorter events, 0.0 us)
Async XLA Ops:
  0.6 4.6 %copy-start.4 = (bf16[32,1536]{1,0:T(8,128)(2,1)S(1)}, bf16[32,1536]{1,0:T(8,128)(2,1)}, u32[]{:S(2)}) copy-start(bf16[32,1536]{1,0:T(8,128)(2,1)} %param.21) | copy-start | bytes 294916
  0.6 4.6 %copy-start = (bf16[1,48,9,512]{3,1,2,0:T(8,128)(2,1)S(1)}, bf16[1,48,9,512]{3,1,2,0:T(8,128)(2,1)}, u32[]{:S(2)}) copy-start(bf16[1,48,9,512]{3,1,2,0:T(8,128)(2,1)} %param.11) | copy-start | bytes 1327108
  5.3 1.0 %copy-start.1 = (bf16[1,48,9,512]{3,1,2,0:T(8,128)(2,1)S(1)}, bf16[1,48,9,512]{3,1,2,0:T(8,128)(2,1)}, u32[]{:S(2)}) copy-start(bf16[1,48,9,512]{3,1,2,0:T(8,128)(2,1)} %param.18) | copy-start | bytes 1327108
  6.3 0.9 %copy-start.2 = (bf16[128,512]{1,0:T(8,128)(2,1)S(1)}, bf16[128,512]{1,0:T(8,128)(2,1)}, u32[]{:S(2)}) copy-start(bf16[128,512]{1,0:T(8,128)(2,1)} %win_ref.1) | copy-start | bytes 393220
  7.2 0.9 %copy-start.3 = (bf16[128,512]{1,0:T(8,128)(2,1)S(1)}, bf16[128,512]{1,0:T(8,128)(2,1)}, u32[]{:S(2)}) copy-start(bf16[128,512]{1,0:T(8,128)(2,1)} %wout_ref.1) | copy-start | bytes 393220

commit v2 on v1

--- a/solution.py
+++ b/solution.py
@@ -110,24 +110,26 @@
             frm = lax.rem(z + zs - j, zs)
             self.arrived(self.rd.at[frm], self.d_s.at[j], self.d_r.at[frm], {"graph": frm})
         if self.split:
-            self.out_ref[...] = self.rd[...].reshape(self.out_ref.shape)
+            self.out_ref[...] = self.rd[...].astype(F32).reshape(self.out_ref.shape)
         else:
             total = self.rd[0].astype(F32)
             for i in range(1, zs):
                 total = total + self.rd[i].astype(F32)
-            self.out_ref[...] = total.astype(BF16)
+            self.out_ref[...] = total
 
 
 def kernel(
     x_count, z_count,
-    feat_ref, cot_ref, geo_ref, frac_ref, win_ref, wout_ref, wrad_ref,
-    new_ref, gf_ref, gin_ref, gout_ref, grad_ref,
-    full_in, full_out, full_rad, feat_pad, frac_pad, proj, rows_e, msg_e, dmsg_e, gates, dgates,
+    feat_ref, cot_hbm, frac_hbm, lattice_hbm, count_hbm, target_hbm, source_hbm, shift_hbm,
+    win_ref, wout_ref, wrad_ref,
+    new_hbm, gf_hbm, gin_hbm, gout_hbm, grad_hbm,
+    new_ref, gf_ref, gin_ref, gout_ref, grad_ref, full_in, full_out, full_rad, feat_pad, frac_pad, proj, rows_e, msg_e, dmsg_e, gates, dgates,
     table, columns, basis_l, basis_r, pre, summed_s, dpre_s, dsum_s, d_pad, rim_lo, rim_hi, dproj_s,
-    w_send, w_recv, h_send, h_recv, *red_scratch,
+    cot_ref, frac_ref, frac_l, frac_r, lattice_ref, count_ref, target_ref, source_ref, shift_ref,
+    w_send, w_recv, h_send, h_recv, load_sem, store_sem, *red_scratch,
 ):
     comps, atoms, channels = feat_ref.shape
-    edges = geo_ref.shape[1]
+    edges = target_ref.shape[1]
     padded = atoms + 2 * RIM
     z = lax.axis_index("graph")
     d = lax.axis_index("dp")
@@ -135,6 +137,35 @@
     peer = 2 * x + 1 - core
     place = dict(core=core, peer=peer, x=x, x_count=x_count, z=z, z_count=z_count)
     sends = []
+    loads = [
+        pltpu.make_async_copy(src, dst, load_sem.at[i])
+        for i, (src, dst) in enumerate(
+            (
+                (feat_ref, feat_pad.at[:, RIM : RIM + atoms]),
+                (win_ref, full_in.at[d]),
+                (wout_ref, full_out.at[d]),
+                (cot_hbm, cot_ref),
+                (frac_hbm, frac_ref),
+                (lattice_hbm, lattice_ref),
+                (count_hbm, count_ref),
+                (target_hbm, target_ref),
+                (source_hbm, source_ref),
+                (shift_hbm, shift_ref),
+            )
+        )
+    ]
+    rad_count, rad_wide = wrad_ref.shape
+    pieces = rad_wide // full_rad.shape[2]
+    rad_loads = [
+        pltpu.make_async_copy(
+            wrad_ref.at[:, i * rad_wide // pieces : (i + 1) * rad_wide // pieces],
+            full_rad.at[d, i * rad_count : (i + 1) * rad_count],
+            load_sem.at[10 + i],
+        )
+        for i in range(pieces)
+    ]
+    for load in loads[4:] + rad_loads + loads[:4]:
+        load.start()
 
     barrier = pltpu.get_barrier_semaphore()
     for j in range(1, z_count):
@@ -162,7 +193,6 @@
             to = 2 * lax.rem(x + j, x_count) + core
             send(w_ref, full.at[d], w_send.at[i, j], w_recv.at[i, d], {"dp": to})
         send(w_ref, full.at[d], w_send.at[i, 0], w_recv.at[i, d], {"dp": peer})
-        full.at[d][...] = w_ref[...]
 
     def gather_forward(i, full):
         for j in range(1, x_count):
@@ -179,36 +209,49 @@
     left = {"graph": lax.rem(z + z_count - 1, z_count)}
     last = atoms - RIM
     ahead = RIM + atoms
-    send(frac_ref.at[last:atoms], frac_pad.at[0:RIM], h_send.at[0], h_recv.at[0], right)
-    send(frac_ref.at[0:RIM], frac_pad.at[ahead:padded], h_send.at[1], h_recv.at[1], left)
+    send(frac_hbm, frac_l, h_send.at[0], h_recv.at[0], right)
+    send(frac_hbm, frac_r, h_send.at[1], h_recv.at[1], left)
     gather_start(0, win_ref, full_in)
     send(feat_ref.at[:, last:atoms], feat_pad.at[:, 0:RIM], h_send.at[2], h_recv.at[2], right)
     send(feat_ref.at[:, 0:RIM], feat_pad.at[:, ahead:padded], h_send.at[3], h_recv.at[3], left)
-    gather_start(1, wrad_ref, full_rad)
-
-    feat_pad[:, RIM:ahead, :] = feat_ref[...]
-    frac_pad[RIM:ahead, :] = frac_ref[...]
-    remote(frac_pad.at[0:RIM], frac_pad.at[0:RIM], h_send.at[0], h_recv.at[0], left).wait_recv()
-    remote(frac_pad.at[ahead:padded], frac_pad.at[ahead:padded], h_send.at[1], h_recv.at[1], right).wait_recv()
-
-    tgt_row = geo_ref[13:14, :]
-    src_row = geo_ref[14:15, :]
+    for load in rad_loads:
+        load.wait()
+    gather_start(1, full_rad.at[d], full_rad)
+
+    for load in loads[4:]:
+        load.wait()
+    remote(frac_l, frac_l, h_send.at[0], h_recv.at[0], left).wait_recv()
+    remote(frac_r, frac_r, h_send.at[1], h_recv.at[1], right).wait_recv()
+    table[...] = jnp.zeros_like(table)
+    for i in range(3):
+        table[i : i + 1, 0:RIM] = frac_l[i, :, last:atoms]
+        table[i : i + 1, RIM:ahead] = frac_ref[i]
+        table[i : i + 1, ahead:padded] = frac_r[i, :, 0:RIM]
+    frac_pad[...] = table[:, 0:128].T
+
+    tgt_row = target_ref[...].astype(F32)
+    total_atoms = z_count * atoms
+    local = source_ref[...] - z * atoms + RIM
+    local = jnp.where(local < 0, local + total_atoms, local)
+    local = jnp.where(local >= total_atoms, local - total_atoms, local)
+    src_row = local.astype(F32)
+    live = lax.broadcasted_iota(jnp.int32, (1, edges), 1) < count_ref[...]
+    live = jnp.where(live, 1.0, 0.0)
     hot_src_t = lax.broadcasted_iota(jnp.int32, (padded, edges), 0).astype(F32) == src_row
     hot_tgt_t = lax.broadcasted_iota(jnp.int32, (atoms, edges), 0).astype(F32) == tgt_row
     diffs = []
     for i in range(3):
-        f_src = jnp.sum(jnp.where(hot_src_t, frac_pad[:, i : i + 1], 0.0), axis=0, keepdims=True)
-        f_tgt = jnp.sum(jnp.where(hot_tgt_t, frac_ref[:, i : i + 1], 0.0), axis=0, keepdims=True)
-        diffs.append(f_src + geo_ref[i : i + 1, :] - f_tgt)
+        f_src = jnp.sum(jnp.where(hot_src_t, frac_pad[0:padded, i : i + 1], 0.0), axis=0, keepdims=True)
+        f_tgt = jnp.sum(jnp.where(hot_tgt_t, frac_pad[RIM:ahead, i : i + 1], 0.0), axis=0, keepdims=True)
+        diffs.append(f_src + shift_ref[i].astype(F32) - f_tgt)
     displace = [
-        sum(diffs[i] * geo_ref[3 + 3 * i + j : 4 + 3 * i + j, :] for i in range(3)) for j in range(3)
+        sum(diffs[i] * lattice_ref[i, :, j : j + 1] for i in range(3)) for j in range(3)
     ]
     distance = jnp.sqrt(
         displace[0] * displace[0] + displace[1] * displace[1] + displace[2] * displace[2] + 1.0
     )
     ux, uy, uz = (displace[j] / distance for j in range(3))
-    envelope = 0.5 * (jnp.cos(math.pi * distance / CUTOFF) + 1.0) * geo_ref[12:13, :]
-    table[...] = jnp.zeros_like(table)
+    envelope = 0.5 * (jnp.cos(math.pi * distance / CUTOFF) + 1.0) * live
     entries = [
         envelope,
         ROOT_THREE * uy,
@@ -246,9 +289,15 @@
     basis_l[...] = jnp.where(half == 0, basis, 0.0).astype(BF16)
     basis_r[...] = jnp.where(half == 1, basis, 0.0).astype(BF16)
 
+    for load in loads[:2]:
+        load.wait()
     gather_forward(0, full_in)
     gather_start(2, wout_ref, full_out)
     gather_forward(1, full_rad)
+    gather_finish(1, full_rad)
+    rad = full_rad[...].reshape(ranks * rad_rows, rad_cols)
+    gates[:, :rad_cols] = dot(basis_l[...], rad)
+    gates[:, rad_cols:] = dot(basis_r[...], rad)
     gather_finish(0, full_in)
     remote(feat_pad.at[:, 0:RIM], feat_pad.at[:, 0:RIM], h_send.at[2], h_recv.at[2], left).wait_recv()
     remote(feat_pad.at[:, ahead:padded], feat_pad.at[:, ahead:padded], h_send.at[3], h_recv.at[3], right).wait_recv()
@@ -259,10 +308,8 @@
     )
     for k in range(comps):
         rows_e[k] = dot(hot_src, proj[k]).astype(BF16)
-    gather_finish(1, full_rad)
-    rad = full_rad[...].reshape(ranks * rad_rows, rad_cols)
-    gates[:, :rad_cols] = dot(basis_l[...], rad)
-    gates[:, rad_cols:] = dot(basis_r[...], rad)
+    for load in loads[2:4]:
+        load.wait()
     gather_forward(2, full_out)
 
     def gate_of(rows):
@@ -289,6 +336,7 @@
     @pl.loop(0, atoms // 16)
     def _(step):
         rows = pl.ds(pl.multiple_of(step * 16, 16), 16)
+        shifted = pl.ds(pl.multiple_of(step * 16 + RIM, 16), 16)
         p0 = pre[0, rows, :]
         gate = jax.nn.sigmoid(p0)
         total = jnp.zeros_like(gate)
@@ -296,12 +344,20 @@
             p = pre[k, rows, :]
             u = cot_ref[k, rows, :].astype(F32)
             total = total + u * p
-            new_ref[k, rows, :] = (feat_ref[k, rows, :].astype(F32) + p * gate).astype(BF16)
+            new_ref[k, rows, :] = (feat_pad[k, shifted, :].astype(F32) + p * gate).astype(BF16)
             if k:
                 dpre_s[k, rows, :] = (u * gate).astype(BF16)
         u0 = cot_ref[0, rows, :].astype(F32)
         dpre_s[0, rows, :] = (u0 * gate + gate * (1.0 - gate) * total).astype(BF16)
 
+    stores = []
+
+    def store(i, src, dst):
+        copy = pltpu.make_async_copy(src, dst, store_sem.at[i])
+        copy.start()
+        stores.append(copy)
+
+    store(0, new_ref, new_hbm)
     scale = 1.0 / (z_count * atoms)
     count = len(red_scratch) // 3
     reds = [
@@ -341,9 +397,20 @@
             d_scalars = d_scalars + gate * mixed
         msg_e[0, rows, :] = d_scalars.astype(BF16)
 
+    red_rad.put(
+        scale
+        * (
+            dot(basis_l[...], dgates[:, :rad_cols], across)
+            + dot(basis_r[...], dgates[:, rad_cols:], across)
+        )
+    )
+    red_rad.stage_a()
     red_out.stage_c()
     for k in range(comps):
         d_pad[k] = dot(hot_src_t, msg_e[k]).astype(BF16)
+    send(d_pad.at[:, 0:RIM], rim_hi, h_send.at[4], h_recv.at[4], left)
+    send(d_pad.at[:, ahead:padded], rim_lo, h_send.at[5], h_recv.at[5], right)
+    red_rad.stage_b()
     red_in.put(
         scale
         * dot(
@@ -353,39 +420,49 @@
         )
     )
     red_in.stage_a()
-    send(d_pad.at[:, 0:RIM], rim_hi, h_send.at[4], h_recv.at[4], left)
-    send(d_pad.at[:, ahead:padded], rim_lo, h_send.at[5], h_recv.at[5], right)
-    red_rad.put(
-        scale
-        * (
-            dot(basis_l[...], dgates[:, :rad_cols], across)
-            + dot(basis_r[...], dgates[:, rad_cols:], across)
-        )
-    )
-    red_rad.stage_a()
+    red_out.stage_d()
     red_in.stage_b()
-    red_rad.stage_b()
-    red_out.stage_d()
+    red_rad.stage_c()
     red_in.stage_c()
-    red_rad.stage_c()
+    red_rad.stage_d()
     remote(rim_hi, rim_hi, h_send.at[4], h_recv.at[4], right).wait_recv()
     remote(rim_lo, rim_lo, h_send.at[5], h_recv.at[5], left).wait_recv()
     dproj_s[...] = d_pad[:, RIM:ahead, :]
     dproj_s[:, 0:RIM, :] = (dproj_s[:, 0:RIM, :].astype(F32) + rim_lo[...].astype(F32)).astype(BF16)
     dproj_s[:, last:atoms, :] = (dproj_s[:, last:atoms, :].astype(F32) + rim_hi[...].astype(F32)).astype(BF16)
-    red_in.stage_d()
-    red_rad.stage_d()
     back = dot(dproj_s[...].reshape(flat), full_in[...].reshape(channels, channels), ((1,), (1,)))
     gf_ref[...] = (
         (cot_ref[...].reshape(flat).astype(F32) + back).astype(BF16).reshape(comps, atoms, channels)
     )
-    for red in reds:
-        red.finish()
+    store(1, gf_ref, gf_hbm)
+    red_in.stage_d()
+    red_out.finish()
+    store(2, gout_ref, gout_hbm)
+    red_rad.finish()
+    for i in range(2):
+        store(
+            3 + i,
+            grad_ref.at[i * quarter : (i + 1) * quarter],
+            grad_hbm.at[:, i * rad_cols : (i + 1) * rad_cols],
+        )
+    red_in.finish()
+    store(5, gin_ref, gin_hbm)
+    for copy in stores:
+        copy.wait()
     for red in reds:
         for copy in red.sends:
             copy.wait_send()
     for copy in sends:
         copy.wait_send()
+
+
+def hand_over(*refs):
+    sem = refs[-1]
+    copies = [pltpu.make_async_copy(refs[i], refs[5 + i], sem.at[i]) for i in range(5)]
+    for copy in copies:
+        copy.start()
+    for copy in copies:
+        copy.wait()
 
 
 def body(x_count, z_count, node_feats, frac_pos, lattice, edge_count, edge_target, edge_source,
@@ -394,32 +471,22 @@
     edges = edge_target.shape[1]
     padded = atoms + 2 * RIM
     dp = 2 * x_count
+    across = lambda array: jnp.transpose(array, (1, 0, 2))
     feats = jnp.transpose(node_feats[0], (1, 0, 2))
     cot = jnp.transpose(cotangent[0], (1, 0, 2))
-    frac = jnp.pad(frac_pos[0].T, ((0, 0), (0, 125)))
-    first = lax.axis_index("graph") * atoms
-    local_src = jnp.mod(edge_source[0] - first + RIM, z_count * atoms)
-    live = jnp.arange(edges, dtype=jnp.int32) < edge_count[0, 0]
-    geo = jnp.concatenate(
-        [
-            edge_shift[0].astype(F32),
-            jnp.broadcast_to(lattice[0].reshape(9, 1), (9, edges)),
-            live.astype(F32)[None],
-            edge_target[0].astype(F32)[None],
-            local_src.astype(F32)[None],
-            jnp.zeros((1, edges), F32),
-        ],
-        axis=0,
-    )
     rad_cols = w_rad.shape[1] // 2
-    rad = jnp.concatenate([w_rad[:, :rad_cols], w_rad[:, rad_cols:]], axis=0)
-    rows, rad_rows = w_in.shape[0], rad.shape[0]
+    rows, rad_rows = w_in.shape[0], 2 * w_rad.shape[0]
+    rad = w_rad
+    if w_rad.shape[0] % 16:
+        rad = jnp.concatenate([w_rad[:, :rad_cols], w_rad[:, rad_cols:]], axis=0)
 
     vmem = lambda shape, dtype=BF16: pltpu.VMEM(shape, dtype)
     dma = pltpu.SemaphoreType.DMA
     scratch = [
+        vmem((comps, atoms, channels)), vmem((comps, atoms, channels)), vmem((rows, channels), F32),
+        vmem((rows, channels), F32), vmem((rad_rows, rad_cols), F32),
         vmem((dp, rows, channels)), vmem((dp, rows, channels)), vmem((dp, rad_rows, rad_cols)),
-        vmem((comps, padded, channels)), vmem((padded, 128), F32), vmem((comps, padded, channels)),
+        vmem((comps, padded, channels)), vmem((128, 128), F32), vmem((comps, padded, channels)),
         vmem((comps, edges, channels)), vmem((comps, edges, channels)), vmem((comps, edges, channels)),
         vmem((edges, 3 * channels), F32), vmem((edges, 3 * channels)),
         vmem((128, edges), F32), vmem((edges, 128), F32), vmem((edges, 2 * RB)), vmem((edges, 2 * RB)),
@@ -427,7 +494,10 @@
         vmem((comps, atoms, channels)), vmem((comps, atoms, channels)),
         vmem((comps, padded, channels)), vmem((comps, RIM, channels)), vmem((comps, RIM, channels)),
         vmem((comps, atoms, channels)),
-        dma((3, 2 * x_count)), dma((3, dp)), dma((6,)), dma((6,)),
+        vmem((comps, atoms, channels)), vmem((3, 1, atoms), F32), vmem((3, 1, atoms), F32), vmem((3, 1, atoms), F32),
+        vmem((3, 1, 3), F32), vmem((1, 1), jnp.int32), vmem((1, edges), jnp.int32),
+        vmem((1, edges), jnp.int32), vmem((3, 1, edges), jnp.int32),
+        dma((3, 2 * x_count)), dma((3, dp)), dma((6,)), dma((6,)), dma((12,)), dma((6,)),
     ]
     for n, cols in ((rows, channels), (rad_rows, rad_cols), (rows, channels)):
         piece = n // z_count if n % (16 * z_count) == 0 else n
@@ -438,32 +508,35 @@
             dma, dma, dma((x_count,)), dma((x_count,)), dma((z_count,)), dma((z_count,)),
             dma((z_count,)), dma((z_count,)),
         ]
-    whole = pl.BlockSpec(memory_space=pltpu.VMEM)
-    new, grad_feats, g_in, g_out, g_rad = pl.pallas_call(
+    outs = [
+        jax.ShapeDtypeStruct((comps, atoms, channels), BF16),
+        jax.ShapeDtypeStruct((comps, atoms, channels), BF16),
+        jax.ShapeDtypeStruct((rows, channels), F32),
+        jax.ShapeDtypeStruct((rows, channels), F32),
+        jax.ShapeDtypeStruct((rad_rows // 2, 2 * rad_cols), F32),
+    ]
+    results = pl.pallas_call(
         functools.partial(kernel, x_count, z_count),
-        out_shape=[
-            jax.ShapeDtypeStruct((comps, atoms, channels), BF16),
-            jax.ShapeDtypeStruct((comps, atoms, channels), BF16),
-            jax.ShapeDtypeStruct((rows, channels), BF16),
-            jax.ShapeDtypeStruct((rows, channels), BF16),
-            jax.ShapeDtypeStruct((rad_rows, rad_cols), BF16),
-        ],
-        in_specs=[whole] * 7,
-        out_specs=[whole] * 5,
+        out_shape=outs,
+        in_specs=[pl.BlockSpec(memory_space=pltpu.HBM)] * 11,
+        out_specs=[pl.BlockSpec(memory_space=pltpu.HBM)] * 5,
         scratch_shapes=scratch,
         compiler_params=pltpu.CompilerParams(
-            collective_id=0, has_side_effects=True, vmem_limit_bytes=50 * 1024 * 1024
+            collective_id=0, has_side_effects=True, vmem_limit_bytes=64 * 1024 * 1024
         ),
-    )(feats, cot, geo, frac, w_in, w_out, rad)
-    g_rad = g_rad.astype(F32)
-    half = rad_rows // 2
-    return (
-        jnp.transpose(new, (1, 0, 2))[None],
-        jnp.transpose(grad_feats, (1, 0, 2))[None],
-        g_in.astype(F32),
-        g_out.astype(F32),
-        jnp.concatenate([g_rad[:half], g_rad[half:]], axis=1),
-    )
+    )(
+        feats, cot, across(frac_pos), across(lattice), edge_count, edge_target, edge_source, across(edge_shift),
+        w_in, w_out, rad,
+    )
+    new, grad_feats, g_in, g_out, g_rad = pl.pallas_call(
+        hand_over,
+        out_shape=outs,
+        in_specs=[pl.BlockSpec(memory_space=pltpu.HBM)] * 5,
+        out_specs=[pl.BlockSpec(memory_space=pltpu.HBM)] * 5,
+        scratch_shapes=[dma((5,))],
+        compiler_params=pltpu.CompilerParams(vmem_limit_bytes=64 * 1024 * 1024),
+    )(*results)
+    return (across(new)[None], across(grad_feats)[None], g_in, g_out, g_rad)
 
 
 def solution(mesh):

time: 60.9 us -> 102 us (1.67)
  Pallas kernels: 48.8 us -> 100 us
  local copies, waits for them, and re-layouts: 5.43 us -> 0 us
  other arithmetic: 4.93 us -> 0 us
    pallas_call x1 -> x2, Pallas kernels: 48.8 us -> 100 us  [the longest x1 50.3 us: body(): pl.pallas_call(functools.partial(kernel, x_count, z_count), out_shape=out...]
    unnamed x13 -> x0, local copies, waits for them, and re-layouts: 5.11 us -> none
    convert_element_type x6 -> x0, other arithmetic: 3.53 us -> none  [the longest x1 0.73 us: body(): g_in.astype(F32)]
where the time goes in v2:
time: 102 us; the launch traced here: 101 us
  Pallas kernels  100 us (98%)
  between operations  1.29 us (1%)
    pallas_call x1, Pallas kernels, body(): pl.pallas_call(functools.partial(kernel, x_count, z_count), out_shape=out...  50.3 us
    pallas_call x1, Pallas kernels, body(): pl.pallas_call(hand_over, out_shape=outs, in_specs=[pl.BlockSpec(memory_s...  49.8 us

profile of v2, /device:TPU:0, one launch (start us, length us, event | category | flops | bytes accessed | tf_op | source)
XLA Modules:
  0.0 101.4 jit_solution(2943446354827779680)
XLA Ops:
  1.3 50.3 %shard_map.146 = (bf16[9,48,512]{2,1,0:T(8,128)(2,1)}, bf16[9,48,512]{2,1,0:T(8,128)(2,1)}, f32[128,512]{1,0:T(8,128)}, f32[128,512]{1,0:T(8,128)}, f32[32,1536]{1,0:T(8,128)}) custom-call(bf16[9,48,512]{2,1,0:T(8,128)(2,1)} %bitcast.15, bf16[9,48,512]{2,1,0:T(8,128)(2,1)} %bitcast.16, f32[3,1,48]{2,1,0:T(1,128)} %bitcast.18, f32[3,1,3]{2,1,0:T(1,128)} %bitcast.19, ...), custom_call_target="tpu_custom_call" | custom-call | tf_op jit(solution)/shard_map/pallas_call | solution.py:518
  51.6 49.8 %shard_map.147 = (bf16[9,48,512]{2,1,0:T(8,128)(2,1)}, bf16[9,48,512]{2,1,0:T(8,128)(2,1)}, f32[128,512]{1,0:T(8,128)}, f32[128,512]{1,0:T(8,128)}, f32[32,1536]{1,0:T(8,128)}) custom-call(bf16[9,48,512]{2,1,0:T(8,128)(2,1)} %get-tuple-element.15.refs_0_, bf16[9,48,512]{2,1,0:T(8,128)(2,1)} %get-tuple-element.16.refs_1_, ...), custom_call_target="tpu_custom_call" | custom-call | tf_op jit(solution)/shard_map/pallas_call | solution.py:531

commit v3 on v2

--- a/solution.py
+++ b/solution.py
@@ -457,12 +457,17 @@
 
 
 def hand_over(*refs):
-    sem = refs[-1]
-    copies = [pltpu.make_async_copy(refs[i], refs[5 + i], sem.at[i]) for i in range(5)]
-    for copy in copies:
-        copy.start()
-    for copy in copies:
-        copy.wait()
+    sources, results, held = refs[:5], refs[5:10], refs[10:15]
+    sem = refs[15]
+    loads = [pltpu.make_async_copy(sources[i], held[i], sem.at[0, i]) for i in range(5)]
+    stores = [pltpu.make_async_copy(held[i], results[i], sem.at[1, i]) for i in range(5)]
+    for load in loads:
+        load.start()
+    for load, store in zip(loads, stores):
+        load.wait()
+        store.start()
+    for store in stores:
+        store.wait()
 
 
 def body(x_count, z_count, node_feats, frac_pos, lattice, edge_count, edge_target, edge_source,
@@ -533,7 +538,7 @@
         out_shape=outs,
         in_specs=[pl.BlockSpec(memory_space=pltpu.HBM)] * 5,
         out_specs=[pl.BlockSpec(memory_space=pltpu.HBM)] * 5,
-        scratch_shapes=[dma((5,))],
+        scratch_shapes=[vmem(out.shape, out.dtype) for out in outs] + [dma((2, 5))],
         compiler_params=pltpu.CompilerParams(vmem_limit_bytes=64 * 1024 * 1024),
     )(*results)
     return (across(new)[None], across(grad_feats)[None], g_in, g_out, g_rad)

time: 102 us -> 54 us (0.53)
  Pallas kernels: 100 us -> 52.6 us
    pallas_call x1, Pallas kernels: 49.8 us -> 2.24 us  [body(): pl.pallas_call(hand_over, out_shape=outs, in_specs=[pl.BlockSpec(memory_s...]
where the time goes in v3:
time: 54 us; the launch traced here: 53.8 us
  Pallas kernels  52.6 us (97%)
  between operations  1.29 us (2%)
    pallas_call x1, Pallas kernels, body(): pl.pallas_call(functools.partial(kernel, x_count, z_count), out_shape=out...  50.3 us
    pallas_call x1, Pallas kernels, body(): pl.pallas_call(hand_over, out_shape=outs, in_specs=[pl.BlockSpec(memory_s...  2.24 us

profile of v3, /device:TPU:0, one launch (start us, length us, event | category | flops | bytes accessed | tf_op | source)
XLA Modules:
  0.0 53.8 jit_solution(9151970969692913161)
XLA Ops:
  1.3 50.3 %shard_map.146 = (bf16[9,48,512]{2,1,0:T(8,128)(2,1)}, bf16[9,48,512]{2,1,0:T(8,128)(2,1)}, f32[128,512]{1,0:T(8,128)}, f32[128,512]{1,0:T(8,128)}, f32[32,1536]{1,0:T(8,128)}) custom-call(bf16[9,48,512]{2,1,0:T(8,128)(2,1)} %bitcast.15, bf16[9,48,512]{2,1,0:T(8,128)(2,1)} %bitcast.16, f32[3,1,48]{2,1,0:T(1,128)} %bitcast.18, f32[3,1,3]{2,1,0:T(1,128)} %bitcast.19, ...), custom_call_target="tpu_custom_call" | custom-call | tf_op jit(solution)/shard_map/pallas_call | solution.py:523
  51.6 2.2 %shard_map.147 = (bf16[9,48,512]{2,1,0:T(8,128)(2,1)}, bf16[9,48,512]{2,1,0:T(8,128)(2,1)}, f32[128,512]{1,0:T(8,128)}, f32[128,512]{1,0:T(8,128)}, f32[32,1536]{1,0:T(8,128)}) custom-call(bf16[9,48,512]{2,1,0:T(8,128)(2,1)} %get-tuple-element.15.refs_0_, bf16[9,48,512]{2,1,0:T(8,128)(2,1)} %get-tuple-element.16.refs_1_, ...), custom_call_target="tpu_custom_call" | custom-call | tf_op jit(solution)/shard_map/pallas_call | solution.py:536

commit v4 on v3

--- a/solution.py
+++ b/solution.py
@@ -217,6 +217,7 @@
     for load in rad_loads:
         load.wait()
     gather_start(1, full_rad.at[d], full_rad)
+    gather_start(2, wout_ref, full_out)
 
     for load in loads[4:]:
         load.wait()
@@ -292,7 +293,6 @@
     for load in loads[:2]:
         load.wait()
     gather_forward(0, full_in)
-    gather_start(2, wout_ref, full_out)
     gather_forward(1, full_rad)
     gather_finish(1, full_rad)
     rad = full_rad[...].reshape(ranks * rad_rows, rad_cols)
@@ -371,7 +371,6 @@
     dsum_s[...] = (
         (0.25 * dot(dpre_s[...].reshape(flat), w_out, ((1,), (1,)))).astype(BF16).reshape(comps, atoms, channels)
     )
-    red_out.stage_b()
     for k in range(comps):
         dmsg_e[k] = dot(hot_tgt, dsum_s[k]).astype(BF16)
 
@@ -397,6 +396,11 @@
             d_scalars = d_scalars + gate * mixed
         msg_e[0, rows, :] = d_scalars.astype(BF16)
 
+    red_out.stage_b()
+    for k in range(comps):
+        d_pad[k] = dot(hot_src_t, msg_e[k]).astype(BF16)
+    send(d_pad.at[:, 0:RIM], rim_hi, h_send.at[4], h_recv.at[4], left)
+    send(d_pad.at[:, ahead:padded], rim_lo, h_send.at[5], h_recv.at[5], right)
     red_rad.put(
         scale
         * (
@@ -405,12 +409,6 @@
         )
     )
     red_rad.stage_a()
-    red_out.stage_c()
-    for k in range(comps):
-        d_pad[k] = dot(hot_src_t, msg_e[k]).astype(BF16)
-    send(d_pad.at[:, 0:RIM], rim_hi, h_send.at[4], h_recv.at[4], left)
-    send(d_pad.at[:, ahead:padded], rim_lo, h_send.at[5], h_recv.at[5], right)
-    red_rad.stage_b()
     red_in.put(
         scale
         * dot(
@@ -420,9 +418,11 @@
         )
     )
     red_in.stage_a()
-    red_out.stage_d()
+    red_rad.stage_b()
+    red_out.stage_c()
     red_in.stage_b()
     red_rad.stage_c()
+    red_out.stage_d()
     red_in.stage_c()
     red_rad.stage_d()
     remote(rim_hi, rim_hi, h_send.at[4], h_recv.at[4], right).wait_recv()

time: 54 us -> 52 us (0.963)
  Pallas kernels: 52.6 us -> 50.5 us
    pallas_call x1, Pallas kernels: 50.3 us -> 48.3 us  [body(): pl.pallas_call(functools.partial(kernel, x_count, z_count), out_shape=out...]
where the time goes in v4:
time: 52 us; the launch traced here: 51.8 us
  Pallas kernels  50.5 us (97%)
  between operations  1.29 us (2%)
    pallas_call x1, Pallas kernels, body(): pl.pallas_call(functools.partial(kernel, x_count, z_count), out_shape=out...  48.3 us
    pallas_call x1, Pallas kernels, body(): pl.pallas_call(hand_over, out_shape=outs, in_specs=[pl.BlockSpec(memory_s...  2.24 us

profile of v4, /device:TPU:0, one launch (start us, length us, event | category | flops | bytes accessed | tf_op | source)
XLA Modules:
  0.0 51.8 jit_solution(6256991298148053016)
XLA Ops:
  1.3 48.3 %shard_map.146 = (bf16[9,48,512]{2,1,0:T(8,128)(2,1)}, bf16[9,48,512]{2,1,0:T(8,128)(2,1)}, f32[128,512]{1,0:T(8,128)}, f32[128,512]{1,0:T(8,128)}, f32[32,1536]{1,0:T(8,128)}) custom-call(bf16[9,48,512]{2,1,0:T(8,128)(2,1)} %bitcast.15, bf16[9,48,512]{2,1,0:T(8,128)(2,1)} %bitcast.16, f32[3,1,48]{2,1,0:T(1,128)} %bitcast.18, f32[3,1,3]{2,1,0:T(1,128)} %bitcast.19, ...), custom_call_target="tpu_custom_call" | custom-call | tf_op jit(solution)/shard_map/pallas_call | solution.py:523
  49.6 2.2 %shard_map.147 = (bf16[9,48,512]{2,1,0:T(8,128)(2,1)}, bf16[9,48,512]{2,1,0:T(8,128)(2,1)}, f32[128,512]{1,0:T(8,128)}, f32[128,512]{1,0:T(8,128)}, f32[32,1536]{1,0:T(8,128)}) custom-call(bf16[9,48,512]{2,1,0:T(8,128)(2,1)} %get-tuple-element.15.refs_0_, bf16[9,48,512]{2,1,0:T(8,128)(2,1)} %get-tuple-element.16.refs_1_, ...), custom_call_target="tpu_custom_call" | custom-call | tf_op jit(solution)/shard_map/pallas_call | solution.py:536

commit v5 on v4

--- a/solution.py
+++ b/solution.py
@@ -221,6 +221,7 @@
 
     for load in loads[4:]:
         load.wait()
+    gather_forward(0, full_in)
     remote(frac_l, frac_l, h_send.at[0], h_recv.at[0], left).wait_recv()
     remote(frac_r, frac_r, h_send.at[1], h_recv.at[1], right).wait_recv()
     table[...] = jnp.zeros_like(table)
@@ -279,6 +280,7 @@
     hot_src_t = hot_src_t.astype(BF16)
     hot_tgt_t = hot_tgt_t.astype(BF16)
 
+    gather_forward(1, full_rad)
     ranks, rad_rows, rad_cols = full_rad.shape
     quarter = rad_rows // 2
     slot = lax.broadcasted_iota(jnp.int32, (1, 2 * RB), 1)
@@ -292,8 +294,6 @@
 
     for load in loads[:2]:
         load.wait()
-    gather_forward(0, full_in)
-    gather_forward(1, full_rad)
     gather_finish(1, full_rad)
     rad = full_rad[...].reshape(ranks * rad_rows, rad_cols)
     gates[:, :rad_cols] = dot(basis_l[...], rad)

time: 52 us -> 52.7 us (1.013)
  Pallas kernels: 50.5 us -> 51.3 us
    pallas_call x1, Pallas kernels: 48.3 us -> 49 us  [body(): pl.pallas_call(functools.partial(kernel, x_count, z_count), out_shape=out...]
where the time goes in v5:
time: 52.7 us; the launch traced here: 52.6 us
  Pallas kernels  51.3 us (97%)
  between operations  1.29 us (2%)
    pallas_call x1, Pallas kernels, body(): pl.pallas_call(functools.partial(kernel, x_count, z_count), out_shape=out...  49 us
    pallas_call x1, Pallas kernels, body(): pl.pallas_call(hand_over, out_shape=outs, in_specs=[pl.BlockSpec(memory_s...  2.24 us

profile of v5, /device:TPU:0, one launch (start us, length us, event | category | flops | bytes accessed | tf_op | source)
XLA Modules:
  0.0 52.6 jit_solution(9658355524628717225)
XLA Ops:
  1.3 49.0 %shard_map.146 = (bf16[9,48,512]{2,1,0:T(8,128)(2,1)}, bf16[9,48,512]{2,1,0:T(8,128)(2,1)}, f32[128,512]{1,0:T(8,128)}, f32[128,512]{1,0:T(8,128)}, f32[32,1536]{1,0:T(8,128)}) custom-call(bf16[9,48,512]{2,1,0:T(8,128)(2,1)} %bitcast.15, bf16[9,48,512]{2,1,0:T(8,128)(2,1)} %bitcast.16, f32[3,1,48]{2,1,0:T(1,128)} %bitcast.18, f32[3,1,3]{2,1,0:T(1,128)} %bitcast.19, ...), custom_call_target="tpu_custom_call" | custom-call | tf_op jit(solution)/shard_map/pallas_call | solution.py:523
  50.3 2.2 %shard_map.147 = (bf16[9,48,512]{2,1,0:T(8,128)(2,1)}, bf16[9,48,512]{2,1,0:T(8,128)(2,1)}, f32[128,512]{1,0:T(8,128)}, f32[128,512]{1,0:T(8,128)}, f32[32,1536]{1,0:T(8,128)}) custom-call(bf16[9,48,512]{2,1,0:T(8,128)(2,1)} %get-tuple-element.15.refs_0_, bf16[9,48,512]{2,1,0:T(8,128)(2,1)} %get-tuple-element.16.refs_1_, ...), custom_call_target="tpu_custom_call" | custom-call | tf_op jit(solution)/shard_map/pallas_call | solution.py:536
